TPU v7x, 32 devices: a whole 2x2x4 slice. The times are simulated.
32 devices in a mesh: group: 2 (over y), gx: 4 (over z), gy: 2 (over x), sec: 2 (over core).
Axes of the slice: x: 2, y: 2, z: 4, core: 2. Of those that a mesh axis runs over, the one named last changes fastest.
Arguments:
- pressure: float32 [2, 32, 32, 128], P('sec', ('group', 'gx'), 'gy'), parts along dimension 1, may hold values from -6 to 6
- pressure_before: float32 [2, 32, 32, 128], P('sec', ('group', 'gx'), 'gy'), parts along dimension 1, may hold values from -6 to 6
- quasi: float32 [2, 32, 32, 128], P('sec', ('group', 'gx'), 'gy'), parts along dimension 1, may hold values from -6 to 6
- quasi_before: float32 [2, 32, 32, 128], P('sec', ('group', 'gx'), 'gy'), parts along dimension 1, may hold values from -6 to 6
- courant: float32 [16, 32, 128], P('gx', 'gy'), may hold values from 0.02 to 0.08
- epsilon: float32 [16, 32, 128], P('gx', 'gy'), may hold values from 0 to 0.3
- delta: float32 [16, 32, 128], P('gx', 'gy'), may hold values from -0.1 to 0.2
- tilt: float32 [16, 32, 128], P('gx', 'gy'), may hold values from -3.140625 to 3.140625
- azimuth: float32 [16, 32, 128], P('gx', 'gy'), may hold values from -3.140625 to 3.140625
- plan: int32 [4], replicated, may hold values from 1 to 8, as said below
- lags: int32 [5], replicated, may hold values from -4 to 4, as said below
Outputs:
- pressure_final: float32 [2, 32, 32, 128], P('sec', ('group', 'gx'), 'gy'), parts along dimension 1
- quasi_final: float32 [2, 32, 32, 128], P('sec', ('group', 'gx'), 'gy'), parts along dimension 1
- image: float32 [5, 32, 32, 128], P(None, ('group', 'gx'), 'gy', 'sec'), parts along dimension 1
There are 2 independent parts, one for each index of `group`. A program takes and returns all parts, laid end to end along the dimension named above; an argument that names none is the same for every part. Nothing has to cross between parts.
Inputs may be any that keep to these rules, and one draw needn't show every extreme that they name: `plan`: distinct steps in rising order; the last entry is 8. Distinct lags; the first is -4 and the last 4.
All inputs are finite; a program needn't handle non-finite values.
Results may differ from a plain program's by a relative error of at most 0.0001.
Values sent between devices are 32-bit elements; how exact they have to be, the bound alone decides.
No kernel may reach another device: no remote copies, remote signals or barrier semaphores. Data moves between devices by JAX's collectives and lax.ppermute only.
A program may use at most 64 MiB of HBM per device.

v0:
```python
import functools

import jax
import jax.numpy as jnp
import numpy as np
from jax import lax
from jax.experimental import pallas as pl
from jax.experimental.pallas import tpu as pltpu
from jax.sharding import PartitionSpec as P

STEPS = 8
REACH = 4
ROWS = 8

SECOND = (-205.0 / 72.0, 8.0 / 5.0, -1.0 / 5.0, 8.0 / 315.0, -1.0 / 560.0)
FIRST = (4.0 / 5.0, -1.0 / 5.0, 4.0 / 105.0, -1.0 / 280.0)
SECOND_TAIL = tuple(c / SECOND[1] for c in SECOND[2:])
FIRST_TAIL = tuple(b / FIRST[0] for b in FIRST[1:])
SECOND_SCALE = 5040.0 / 8192.0
FIRST_SCALE = 840.0 / 1024.0


def depth_matrix(depth):
    second = np.zeros((depth, depth))
    first = np.zeros((depth, depth))
    for m in range(1, REACH + 1):
        second += SECOND_SCALE * SECOND[m] * (np.eye(depth, k=m) + np.eye(depth, k=-m))
        first += FIRST_SCALE * FIRST[m - 1] * (np.eye(depth, k=-m) - np.eye(depth, k=m))
    both = np.concatenate([second, first], axis=1)
    return jnp.asarray(np.concatenate([both, both], axis=0), jnp.bfloat16)


def swapped(block, axis, bit):
    count = lax.axis_size(axis)
    return lax.ppermute(block, axis, [(i, i ^ bit) for i in range(count)])


def window(place, tile, halo, total, unit):
    count = total // tile
    length = 0
    for i in range(count):
        low = max(0, i * tile - halo) // unit * unit
        high = -(-min(total, (i + 1) * tile + halo) // unit) * unit
        length = max(length, high - low)
    start = jnp.clip((place * tile - halo) // unit * unit, 0, total - length)
    return start, length


def pair_sums(load, tail):
    total = load(1) + load(-1)
    for m, c in enumerate(tail, 2):
        total = total + c * (load(m) + load(-m))
    return total


def pair_differences(load, tail):
    total = load(1) - load(-1)
    for m, b in enumerate(tail, 2):
        total = total + b * (load(m) - load(-m))
    return total


def steps_kernel(sizes, plan_ref, place_ref, matrix_ref, *refs):
    tile_x, tile_y, total_x, total_y, depth, slots, nsnap = sizes
    tiles = refs[: len(slots)]
    halves = refs[len(slots)]
    p_out, q_out, snap_out = refs[len(slots) + 1 : len(slots) + 4]
    pa, pb, qa, qb, first_z, second_z, slope_x, weights = refs[len(slots) + 4 :]
    gx, gy, sec = place_ref[0], place_ref[1], place_ref[2]
    half = tile_x // 2

    full_y = total_y + 2 * ROWS
    for ref in (pa, pb, qa, qb, first_z.at[0], first_z.at[1]):
        for start in (0, total_x + REACH):
            ref[start : start + REACH] = jnp.zeros((REACH, full_y, depth), jnp.float32)
        for start in (0, total_y + ROWS):
            ref[:, start : start + ROWS] = jnp.zeros((total_x + 2 * REACH, ROWS, depth), jnp.float32)
    for start in (0, total_y + ROWS):
        slope_x[:, start : start + ROWS] = jnp.zeros((2, ROWS, depth), jnp.float32)

    for slot, (kx, ky) in enumerate(slots):
        ix, iy = jnp.bitwise_xor(gx, kx), jnp.bitwise_xor(gy, ky)
        xs = ix * tile_x
        ys = pl.multiple_of(iy * tile_y, ROWS)
        for number, ref in enumerate((pa, pb, qa, qb)):
            ref[pl.ds(xs + REACH, tile_x), pl.ds(pl.multiple_of(ys + ROWS, ROWS), tile_y)] = tiles[slot][
                number * tile_x : (number + 1) * tile_x
            ]
        for side in (0, 1):
            source = halves.at[slot] if side else tiles[slot].at[4 * tile_x :]
            base = xs + half * (jnp.bitwise_xor(sec, side))
            for row in range(half):
                courant, epsilon, delta, tilt, azimuth = (source[g * half + row] for g in range(5))
                sin_t, cos_t = jnp.sin(tilt), jnp.cos(tilt)
                sin_a, cos_a = jnp.sin(azimuth), jnp.cos(azimuth)
                axis_x, axis_y = sin_t * cos_a, sin_t * sin_a
                cross = courant * (2.0 * FIRST[0] / FIRST_SCALE)
                fields = (
                    courant * SECOND[1] * axis_x * axis_x,
                    courant * SECOND[1] * axis_y * axis_y,
                    courant * (1.0 / SECOND_SCALE) * cos_t * cos_t,
                    courant * (2.0 * FIRST[0] * FIRST[0]) * axis_x * axis_y,
                    cross * axis_y * cos_t,
                    cross * axis_x * cos_t,
                    courant * SECOND[1],
                    1.0 + 2.0 * epsilon,
                    1.0 + 2.0 * delta,
                )
                for number, field in enumerate(fields):
                    weights[number, base + row, pl.ds(ys, tile_y)] = field

    matrix = matrix_ref[...]
    now, before = (pa, qa), (pb, qb)
    for step in range(1, STEPS + 1):
        left = REACH * (STEPS - step)
        x_low = jnp.maximum(gx * tile_x - left - REACH, 0)
        x_high = jnp.minimum((gx + 1) * tile_x + left + REACH, total_x)
        y_low, y_length = window(gy, tile_y, left, total_y, ROWS)
        if y_length == total_y:
            y_low = 0
        slope_length = min(y_length + 2 * ROWS, total_y)
        slope_low = 0 if slope_length == total_y else jnp.clip(y_low - ROWS, 0, total_y - slope_length)
        z_low = jnp.maximum(x_low - REACH, 0) // REACH
        z_high = jnp.minimum(x_high + REACH, total_x) // REACH

        def depth_body(block, carry, now=now):
            x = block * REACH
            rows = REACH * total_y
            parts = [
                ref[pl.ds(x + REACH, REACH), ROWS : ROWS + total_y].reshape(rows, depth) for ref in now
            ]
            both = jnp.concatenate(parts, axis=0)
            high = both.astype(jnp.bfloat16)
            low = (both - high.astype(jnp.float32)).astype(jnp.bfloat16)
            out = jnp.dot(
                jnp.concatenate([high, low], axis=1), matrix, preferred_element_type=jnp.float32
            )
            for f in (0, 1):
                piece = out[f * rows : (f + 1) * rows]
                second_z[f, pl.ds(x, REACH)] = piece[:, :depth].reshape(REACH, total_y, depth)
                first_z[f, pl.ds(x + REACH, REACH), ROWS : ROWS + total_y] = piece[:, depth:].reshape(
                    REACH, total_y, depth
                )
            return carry

        lax.fori_loop(z_low, z_high, depth_body, 0)

        def row_body(x, carry, now=now, before=before, y_low=y_low, y_length=y_length,
                     slope_low=slope_low, slope_length=slope_length):
            row = x + REACH
            for f in (0, 1):
                for j in range(0, slope_length, ROWS):
                    ys = pl.ds(ROWS + slope_low + j, ROWS)
                    load = lambda m: now[f][row + m, ys]
                    slope_x[f, ys] = pair_differences(load, FIRST_TAIL)
            for j in range(0, y_length, ROWS):
                at = y_low + j
                ys = pl.ds(at, ROWS)
                here = ROWS + at
                w = [weights[i, x, ys] for i in range(9)]
                axial = []
                for f in (0, 1):
                    along_x = lambda m: now[f][row + m, pl.ds(here, ROWS)]
                    along_y = lambda m: now[f][row, pl.ds(here + m, ROWS)]
                    curve_xx = pair_sums(along_x, SECOND_TAIL)
                    curve_yy = pair_sums(along_y, SECOND_TAIL)
                    curve_zz = second_z[f, x, ys]
                    curve_xy = pair_differences(lambda m: slope_x[f, pl.ds(here + m, ROWS)], FIRST_TAIL)
                    curve_yz = pair_differences(
                        lambda m: first_z[f, row, pl.ds(here + m, ROWS)], FIRST_TAIL
                    )
                    curve_xz = pair_differences(
                        lambda m: first_z[f, row + m, pl.ds(here, ROWS)], FIRST_TAIL
                    )
                    axial.append(
                        w[0] * curve_xx + w[1] * curve_yy + w[2] * curve_zz
                        + w[3] * curve_xy + w[4] * curve_yz + w[5] * curve_xz
                    )
                    if f == 0:
                        laplace = curve_xx + curve_yy + curve_zz * (1.0 / (SECOND_SCALE * SECOND[1]))
                p = now[0][row, pl.ds(here, ROWS)]
                q = now[1][row, pl.ds(here, ROWS)]
                flat = w[6] * (laplace + (2.0 * SECOND[0] / SECOND[1]) * p) - axial[0]
                shared = axial[1] + w[6] * ((SECOND[0] / SECOND[1]) * q)
                spot = (row, pl.ds(here, ROWS))
                before[0][spot] = 2.0 * p - before[0][spot] + w[7] * flat + shared
                before[1][spot] = 2.0 * q - before[1][spot] + w[8] * flat + shared
            return carry

        lax.fori_loop(x_low, x_high, row_body, 0)
        now, before = before, now

        mine = pl.ds(pl.multiple_of(ROWS + gy * tile_y, ROWS), tile_y)
        for j in range(nsnap):
            @pl.when(plan_ref[j] == step)
            def _():
                snap_out[j] = now[0][pl.ds(gx * tile_x, tile_x + 2 * REACH), mine]

    p_out[0] = now[0][pl.ds(gx * tile_x + REACH, tile_x), mine]
    q_out[0] = now[1][pl.ds(gx * tile_x + REACH, tile_x), mine]


def image_kernel(lags_ref, place_ref, own_ref, other_ref, image_ref):
    sec = place_ref[2]
    sign = 1 - 2 * sec
    nlag, tile_x, tile_y, half = image_ref.shape
    nsnap = own_ref.shape[0]
    for k in range(nlag):
        shift = sign * lags_ref[k]
        total = own_ref[0, pl.ds(REACH - shift, tile_x)] * other_ref[0, pl.ds(REACH + shift, tile_x)]
        for j in range(1, nsnap):
            total = total + own_ref[j, pl.ds(REACH - shift, tile_x)] * other_ref[j, pl.ds(REACH + shift, tile_x)]
        flat = total.reshape(tile_x * tile_y, 2 * half)
        chosen = jnp.where(sec == 0, flat, pltpu.roll(flat, half, 1))
        image_ref[k] = chosen[:, :half].reshape(tile_x, tile_y, half)


def gathered_solution(pressure, pressure_before, quasi, quasi_before, courant, epsilon, delta, tilt, azimuth, plan, lags):
    count_x, count_y = lax.axis_size("gx"), lax.axis_size("gy")
    gx, gy, sec = lax.axis_index("gx"), lax.axis_index("gy"), lax.axis_index("sec")
    _, tile_x, tile_y, depth = pressure.shape
    total_x, total_y = count_x * tile_x, count_y * tile_y
    half = tile_x // 2
    place = jnp.stack([gx, gy, sec]).astype(jnp.int32)

    waves = jnp.concatenate([pressure[0], pressure_before[0], quasi[0], quasi_before[0]])
    earth = jnp.stack([courant, epsilon, delta, tilt, azimuth])
    earth = lax.dynamic_slice_in_dim(earth, sec * half, half, 1).reshape(5 * half, tile_y, depth)
    held = {(0, 0): jnp.concatenate([waves, earth])}
    for ky in range(count_y):
        if ky:
            low = ky & -ky
            held[0, ky] = swapped(held[0, ky ^ low], "gy", low)
    for kx in range(1, count_x):
        low = kx & -kx
        rest = kx ^ low
        held[kx, 0] = swapped(held[rest, 0] if rest else held[0, 0], "gx", low)
    for kx in range(1, count_x):
        for ky in range(1, count_y):
            low = ky & -ky
            held[kx, ky] = swapped(held[kx, ky ^ low], "gy", low)
    slots = tuple(held)
    tiles = list(held.values())
    other = swapped(jnp.stack([t[4 * tile_x :] for t in tiles]), "sec", 1)

    nsnap = plan.shape[0]
    sizes = (tile_x, tile_y, total_x, total_y, depth, slots, nsnap)
    vmem = pl.BlockSpec(memory_space=pltpu.VMEM)
    smem = pl.BlockSpec(memory_space=pltpu.SMEM)
    field = pltpu.VMEM((total_x + 2 * REACH, total_y + 2 * ROWS, depth), jnp.float32)
    p_final, q_final, snaps = pl.pallas_call(
        functools.partial(steps_kernel, sizes),
        out_shape=(
            jax.ShapeDtypeStruct(pressure.shape, jnp.float32),
            jax.ShapeDtypeStruct(quasi.shape, jnp.float32),
            jax.ShapeDtypeStruct((nsnap, tile_x + 2 * REACH, tile_y, depth), jnp.float32),
        ),
        in_specs=[smem, smem, vmem] + [vmem] * (len(tiles) + 1),
        out_specs=(vmem, vmem, vmem),
        scratch_shapes=[
            field, field, field, field,
            pltpu.VMEM((2, total_x + 2 * REACH, total_y + 2 * ROWS, depth), jnp.float32),
            pltpu.VMEM((2, total_x, total_y, depth), jnp.float32),
            pltpu.VMEM((2, total_y + 2 * ROWS, depth), jnp.float32),
            pltpu.VMEM((9, total_x, total_y, depth), jnp.float32),
        ],
        compiler_params=pltpu.CompilerParams(vmem_limit_bytes=40 * 1024 * 1024),
    )(plan, place, depth_matrix(depth), *tiles, other)

    other_snaps = swapped(snaps, "sec", 1)
    image = pl.pallas_call(
        image_kernel,
        out_shape=jax.ShapeDtypeStruct((lags.shape[0], tile_x, tile_y, depth // 2), jnp.float32),
        in_specs=[smem, smem, vmem, vmem],
        out_specs=vmem,
    )(lags, place, snaps, other_snaps)
    return (p_final, q_final, image)


def with_halo(cells, sides, width):
    for axis, dim in sides:
        count = lax.axis_size(axis)
        ends = count - 1
        head = lax.slice_in_dim(cells, 0, width, axis=dim)
        tail = lax.slice_in_dim(cells, cells.shape[dim] - width, cells.shape[dim], axis=dim)
        cells = jnp.concatenate(
            [
                lax.ppermute(tail, axis, [(i, (i + 1) % count) for i in range(ends)]),
                cells,
                lax.ppermute(head, axis, [((i + 1) % count, i) for i in range(ends)]),
            ],
            axis=dim,
        )
    return cells


def from_behind(block, axis, distance):
    devices = range(lax.axis_size(axis))
    route = [(i - distance, i) for i in devices if i - distance in devices]
    return lax.ppermute(block, axis, route)


def second_along(values, dimension):
    amount = values.shape[dimension] - 8
    result = SECOND[0] * lax.slice_in_dim(values, 4, 4 + amount, axis=dimension)
    for offset in range(1, 5):
        result = result + SECOND[offset] * (
            lax.slice_in_dim(values, 4 + offset, 4 + offset + amount, axis=dimension)
            + lax.slice_in_dim(values, 4 - offset, 4 - offset + amount, axis=dimension)
        )
    return result


def first_along(values, dimension):
    amount = values.shape[dimension] - 8
    result = FIRST[0] * (
        lax.slice_in_dim(values, 5, 5 + amount, axis=dimension)
        - lax.slice_in_dim(values, 3, 3 + amount, axis=dimension)
    )
    for offset in range(2, 5):
        result = result + FIRST[offset - 1] * (
            lax.slice_in_dim(values, 4 + offset, 4 + offset + amount, axis=dimension)
            - lax.slice_in_dim(values, 4 - offset, 4 - offset + amount, axis=dimension)
        )
    return result


def trimmed(values, dimensions):
    for dimension in dimensions:
        values = lax.slice_in_dim(values, 4, values.shape[dimension] - 4, axis=dimension)
    return values


def orientation(tilt, azimuth):
    sin_tilt = jnp.sin(tilt)
    cos_tilt = jnp.cos(tilt)
    sin_azim = jnp.sin(azimuth)
    cos_azim = jnp.cos(azimuth)
    square_sin = sin_tilt * sin_tilt
    double_tilt = jnp.sin(2.0 * tilt)
    return (
        square_sin * cos_azim * cos_azim,
        square_sin * sin_azim * sin_azim,
        cos_tilt * cos_tilt,
        square_sin * jnp.sin(2.0 * azimuth),
        double_tilt * sin_azim,
        double_tilt * cos_azim,
    )


def tilted_terms(padded, weights):
    curve_xx = trimmed(second_along(padded, 1), (2, 3))
    curve_yy = trimmed(second_along(padded, 2), (1, 3))
    curve_zz = trimmed(second_along(padded, 3), (1, 2))
    slope_x = first_along(padded, 1)
    slope_y = first_along(padded, 2)
    curve_xy = trimmed(first_along(slope_x, 2), (3,))
    curve_xz = trimmed(first_along(slope_x, 3), (2,))
    curve_yz = trimmed(first_along(slope_y, 3), (1,))
    axial = (
        weights[0] * curve_xx
        + weights[1] * curve_yy
        + weights[2] * curve_zz
        + weights[3] * curve_xy
        + weights[4] * curve_yz
        + weights[5] * curve_xz
    )
    laplace = curve_xx + curve_yy + curve_zz
    return (axial, laplace)


def advance(now_p, before_p, now_q, before_q, axial_p, laplace_p, axial_q, courant, epsilon, delta):
    flat_p = laplace_p - axial_p
    next_p = 2.0 * now_p - before_p + courant * ((1.0 + 2.0 * epsilon) * flat_p + axial_q)
    next_q = 2.0 * now_q - before_q + courant * ((1.0 + 2.0 * delta) * flat_p + axial_q)
    return (next_p, next_q)


def offset_image(paired, lags):
    rim_width = paired.shape[2]
    padded = with_halo(paired, (("gx", 2),), rim_width)
    images = []
    for offset_index in range(lags.shape[0]):
        lag_cells = lags[offset_index]
        source = lax.dynamic_slice_in_dim(padded[0], rim_width - lag_cells, rim_width, 1)
        receiver = lax.dynamic_slice_in_dim(padded[1], rim_width + lag_cells, rim_width, 1)
        images.append(jnp.sum(source * receiver, axis=0))
    return jnp.stack(images)


def stepwise_solution(pressure, pressure_before, quasi, quasi_before, courant, epsilon, delta, tilt, azimuth, plan, lags):
    weights = orientation(tilt, azimuth)
    snapshots = jnp.zeros((plan.shape[0],) + pressure.shape[1:], jnp.float32)
    for step in range(STEPS):
        stacked = jnp.concatenate([pressure, quasi], 0)
        padded = with_halo(stacked, (("gx", 1), ("gy", 2)), 4)
        padded = jnp.pad(padded, ((0, 0), (0, 0), (0, 0), (4, 4)))
        axial, laplace = tilted_terms(padded, weights)
        next_p, next_q = advance(
            pressure, pressure_before, quasi, quasi_before,
            axial[0:1], laplace[0:1], axial[1:2], courant, epsilon, delta,
        )
        pressure_before, quasi_before = (pressure, quasi)
        pressure, quasi = (next_p, next_q)
        picked = (plan == step + 1).astype(jnp.float32)
        snapshots = snapshots + picked[:, None, None, None] * pressure
    arrived = from_behind(snapshots, "sec", 1)
    paired = jnp.stack([arrived, snapshots])
    whole_image = offset_image(paired, lags)
    half_depth = whole_image.shape[3] // 2
    returned = from_behind(whole_image[..., :half_depth], "sec", -1)
    image = jnp.where(lax.axis_index("sec") == 0, returned, whole_image[..., half_depth:])
    return (pressure, quasi, image)


def on_device(*args):
    count_x, count_y = lax.axis_size("gx"), lax.axis_size("gy")
    _, tile_x, tile_y, depth = args[0].shape
    cells = count_x * tile_x * count_y * tile_y * depth
    fits = (
        cells <= 1 << 17
        and count_x & (count_x - 1) == 0
        and count_y & (count_y - 1) == 0
        and tile_x % REACH == 0
        and tile_y % ROWS == 0
        and depth == 128
    )
    return (gathered_solution if fits else stepwise_solution)(*args)


def solution(mesh):
    wave = P("sec", ("group", "gx"), "gy", None)
    earth = P("gx", "gy", None)
    return jax.shard_map(
        on_device,
        mesh=mesh,
        in_specs=(wave,) * 4 + (earth,) * 5 + (P(), P()),
        out_specs=(wave, wave, P(None, ("group", "gx"), "gy", "sec")),
        check_vma=False,
    )
```

profile of v0, /device:TPU:0, one launch (start us, length us, event | category | flops | bytes accessed | tf_op | source)
XLA Modules:
  0.0 67.2 jit_solution(4505217036141694415)
XLA Ops:
  0.6 0.8 %constant_dynamic-update-slice_fusion.4 = f32[5,4,16,128]{3,2,1,0:T(8,128)S(1)} fusion(f32[4,16,128]{2,1,0:T(8,128)} %param.16), kind=kLoop, calls=%fused_computation.19 | loop fusion | bytes 65536
  1.4 0.8 %copy-done.6 = f32[4,16,128]{2,1,0:T(8,128)S(1)} copy-done((f32[4,16,128]{2,1,0:T(8,128)S(1)}, f32[4,16,128]{2,1,0:T(8,128)}, u32[]{:S(2)}) %copy-start.6) | copy-done | bytes 32792
  2.2 0.8 %copy-done.7 = f32[4,16,128]{2,1,0:T(8,128)S(1)} copy-done((f32[4,16,128]{2,1,0:T(8,128)S(1)}, f32[4,16,128]{2,1,0:T(8,128)}, u32[]{:S(2)}) %copy-start.7) | copy-done | bytes 32792
  2.9 0.8 %copy-done.8 = f32[4,16,128]{2,1,0:T(8,128)S(1)} copy-done((f32[4,16,128]{2,1,0:T(8,128)S(1)}, f32[4,16,128]{2,1,0:T(8,128)}, u32[]{:S(2)}) %copy-start.8) | copy-done | bytes 32792
  3.7 0.8 %copy-done.9 = f32[4,16,128]{2,1,0:T(8,128)S(1)} copy-done((f32[4,16,128]{2,1,0:T(8,128)S(1)}, f32[4,16,128]{2,1,0:T(8,128)}, u32[]{:S(2)}) %copy-start.9) | copy-done | bytes 32792
  4.5 0.7 %copy-done.10 = f32[1,4,16,128]{3,2,1,0:T(8,128)S(1)} copy-done((f32[1,4,16,128]{3,2,1,0:T(8,128)S(1)}, f32[1,4,16,128]{3,2,1,0:T(8,128)}, u32[]{:S(2)}) %copy-start.10) | copy-done | bytes 32792
  5.2 0.8 %copy-done.11 = f32[1,4,16,128]{3,2,1,0:T(8,128)S(1)} copy-done((f32[1,4,16,128]{3,2,1,0:T(8,128)S(1)}, f32[1,4,16,128]{3,2,1,0:T(8,128)}, u32[]{:S(2)}) %copy-start.11) | copy-done | bytes 32792
  6.0 0.8 %copy-done.12 = f32[1,4,16,128]{3,2,1,0:T(8,128)S(1)} copy-done((f32[1,4,16,128]{3,2,1,0:T(8,128)S(1)}, f32[1,4,16,128]{3,2,1,0:T(8,128)}, u32[]{:S(2)}) %copy-start.12) | copy-done | bytes 32792
  6.7 4.1 %collective-permute-start.2 = (f32[26,16,128]{2,1,0:T(8,128)S(1)}, f32[26,16,128]{2,1,0:T(8,128)S(1)}, u32[]{:S(2)}, u32[]{:S(2)}) collective-permute-start(f32[26,16,128]{2,1,0:T(8,128)S(1)} %constant_dynamic-update-slice_fusion.5.refs_0_), channel_id=1, source_target_pairs={{0,8},{4,12},{8,0},{12,4},{1,9},{5,13},{9,1},{13,5},{2,10},{6,14},... | collective-permute-start | bytes 638984 | tf_op jit(solution)/shard_map/ppermute | solution.py:35
  10.8 1.6 %collective-permute-start.1 = (f32[26,16,128]{2,1,0:T(8,128)S(1)}, f32[26,16,128]{2,1,0:T(8,128)S(1)}, u32[]{:S(2)}, u32[]{:S(2)}) collective-permute-start(f32[26,16,128]{2,1,0:T(8,128)S(1)} %constant_dynamic-update-slice_fusion.5.refs_0_), channel_id=1, source_target_pairs={{0,4},{4,0},{8,12},{12,8},{1,5},{5,1},{9,13},{13,9},{2,6},{6,2},{1... | collective-permute-start | bytes 638984 | tf_op jit(solution)/shard_map/ppermute | solution.py:35
  12.4 1.5 %collective-permute-start = (f32[26,16,128]{2,1,0:T(8,128)S(1)}, f32[26,16,128]{2,1,0:T(8,128)S(1)}, u32[]{:S(2)}, u32[]{:S(2)}) collective-permute-start(f32[26,16,128]{2,1,0:T(8,128)S(1)} %constant_dynamic-update-slice_fusion.5.refs_0_), channel_id=1, source_target_pairs={{0,2},{2,0},{1,3},{3,1},{4,6},{6,4},{5,7},{7,5},{8,10},{10,8},{9,1... | collective-permute-start | bytes 638984 | tf_op jit(solution)/shard_map/ppermute | solution.py:35
  13.9 6.8 %collective-permute-done.2.refs_3_ = f32[26,16,128]{2,1,0:T(8,128)S(1)} collective-permute-done((f32[26,16,128]{2,1,0:T(8,128)S(1)}, f32[26,16,128]{2,1,0:T(8,128)S(1)}, u32[]{:S(2)}, u32[]{:S(2)}) %collective-permute-start.2) | collective-permute-done | bytes 213024 | tf_op jit(solution)/shard_map/ppermute | solution.py:35
  20.8 1.5 %collective-permute-start.5 = (f32[26,16,128]{2,1,0:T(8,128)S(1)}, f32[26,16,128]{2,1,0:T(8,128)S(1)}, u32[]{:S(2)}, u32[]{:S(2)}) collective-permute-start(f32[26,16,128]{2,1,0:T(8,128)S(1)} %collective-permute-done.2.refs_3_), channel_id=1, source_target_pairs={{0,2},{2,0},{1,3},{3,1},{4,6},{6,4},{5,7},{7,5},{8,10},{10,8},{9,1... | collective-permute-start | bytes 638984 | tf_op jit(solution)/shard_map/ppermute | solution.py:35
  22.3 0.6 collective-permute-start.3
  22.9 0.5 collective-permute-start.4
  23.5 4.7 %collective-permute-done.3.refs_4_ = f32[26,16,128]{2,1,0:T(8,128)S(1)} collective-permute-done((f32[26,16,128]{2,1,0:T(8,128)S(1)}, f32[26,16,128]{2,1,0:T(8,128)S(1)}, u32[]{:S(2)}, u32[]{:S(2)}) %collective-permute-start.3) | collective-permute-done | bytes 213024 | tf_op jit(solution)/shard_map/ppermute | solution.py:35
  28.2 0.7 %collective-permute-start.6 = (f32[26,16,128]{2,1,0:T(8,128)S(1)}, f32[26,16,128]{2,1,0:T(8,128)S(1)}, u32[]{:S(2)}, u32[]{:S(2)}) collective-permute-start(f32[26,16,128]{2,1,0:T(8,128)S(1)} %collective-permute-done.3.refs_4_), channel_id=1, source_target_pairs={{0,2},{2,0},{1,3},{3,1},{4,6},{6,4},{5,7},{7,5},{8,10},{10,8},{9,1... | collective-permute-start | bytes 638984 | tf_op jit(solution)/shard_map/ppermute | solution.py:35
  28.9 4.6 %collective-permute-done.4.refs_5_ = f32[26,16,128]{2,1,0:T(8,128)S(1)} collective-permute-done((f32[26,16,128]{2,1,0:T(8,128)S(1)}, f32[26,16,128]{2,1,0:T(8,128)S(1)}, u32[]{:S(2)}, u32[]{:S(2)}) %collective-permute-start.4) | collective-permute-done | bytes 213024 | tf_op jit(solution)/shard_map/ppermute | solution.py:35
  33.6 2.7 %collective-permute-done.6.refs_7_ = f32[26,16,128]{2,1,0:T(8,128)S(1)} collective-permute-done((f32[26,16,128]{2,1,0:T(8,128)S(1)}, f32[26,16,128]{2,1,0:T(8,128)S(1)}, u32[]{:S(2)}, u32[]{:S(2)}) %collective-permute-start.6) | collective-permute-done | bytes 213024 | tf_op jit(solution)/shard_map/ppermute | solution.py:35
  36.5 2.0 %collective-permute-done.7.refs_8_ = f32[8,10,16,128]{3,2,1,0:T(8,128)S(1)} collective-permute-done((f32[8,10,16,128]{3,2,1,0:T(8,128)S(1)}, f32[8,10,16,128]{3,2,1,0:T(8,128)S(1)}, u32[]{:S(2)}, u32[]{:S(2)}) %collective-permute-start.7) | collective-permute-done | bytes 655392 | tf_op jit(solution)/shard_map/ppermute | solution.py:35
  38.4 24.3 %shard_map.139 = (f32[1,4,16,128]{3,2,1,0:T(8,128)}, f32[1,4,16,128]{3,2,1,0:T(8,128)}, f32[4,12,16,128]{3,2,1,0:T(8,128)S(1)}) custom-call(s32[4]{0:T(128)S(1)} %copy-done.3, s32[3]{0:T(128)S(1)} %pad_add_fusion.place_ref, bf16[256,256]{1,0:T(8,128)(2,1)S(1)} %copy-done.1, f32[26,16,128]{2,1,0:T(8,128)S(1)} %constant_dynamic-update-slice_fusion.5.refs_0_, ...), custom_call_target="tpu_custom_call" | custom-call | tf_op jit(solution)/shard_map/pallas_call | solution.py:251
  62.9 1.6 %collective-permute-done.8.other_ref = f32[4,12,16,128]{3,2,1,0:T(8,128)S(1)} collective-permute-done((f32[4,12,16,128]{3,2,1,0:T(8,128)S(1)}, f32[4,12,16,128]{3,2,1,0:T(8,128)S(1)}, u32[]{:S(2)}, u32[]{:S(2)}) %collective-permute-start.8) | collective-permute-done | bytes 393248 | tf_op jit(solution)/shard_map/ppermute | solution.py:35
  64.5 0.7 %copy-done.4 = f32[4,12,16,128]{3,2,1,0:T(8,128)} copy-done((f32[4,12,16,128]{3,2,1,0:T(8,128)}, f32[4,12,16,128]{3,2,1,0:T(8,128)S(1)}, u32[]{:S(2)}) %copy-start.4) | copy-done | bytes 393240
  65.2 1.9 %shard_map.140 = f32[5,4,16,64]{3,2,1,0:T(8,128)} custom-call(s32[5]{0:T(128)} %lags_ref.1, s32[3]{0:T(128)} %copy-done.2, f32[4,12,16,128]{3,2,1,0:T(8,128)} %copy-done, f32[4,12,16,128]{3,2,1,0:T(8,128)} %copy-done.4), custom_call_target="tpu_custom_call" | custom-call | tf_op jit(solution)/shard_map/pallas_call | solution.py:271
  (42 shorter events, 0.4 us)
Async XLA Ops:
  0.6 0.8 %copy-start.5 = (f32[1,4,16,128]{3,2,1,0:T(8,128)S(1)}, f32[1,4,16,128]{3,2,1,0:T(8,128)}, u32[]{:S(2)}) copy-start(f32[1,4,16,128]{3,2,1,0:T(8,128)} %param.12) | copy-start | bytes 98308
  1.4 0.8 %copy-start.6 = (f32[4,16,128]{2,1,0:T(8,128)S(1)}, f32[4,16,128]{2,1,0:T(8,128)}, u32[]{:S(2)}) copy-start(f32[4,16,128]{2,1,0:T(8,128)} %param.17) | copy-start | bytes 98308
  2.2 0.8 %copy-start.7 = (f32[4,16,128]{2,1,0:T(8,128)S(1)}, f32[4,16,128]{2,1,0:T(8,128)}, u32[]{:S(2)}) copy-start(f32[4,16,128]{2,1,0:T(8,128)} %param.18) | copy-start | bytes 98308
  2.9 0.8 %copy-start.8 = (f32[4,16,128]{2,1,0:T(8,128)S(1)}, f32[4,16,128]{2,1,0:T(8,128)}, u32[]{:S(2)}) copy-start(f32[4,16,128]{2,1,0:T(8,128)} %param.19) | copy-start | bytes 98308
  3.7 0.8 %copy-start.9 = (f32[4,16,128]{2,1,0:T(8,128)S(1)}, f32[4,16,128]{2,1,0:T(8,128)}, u32[]{:S(2)}) copy-start(f32[4,16,128]{2,1,0:T(8,128)} %param.20) | copy-start | bytes 98308
  4.5 0.8 %copy-start.10 = (f32[1,4,16,128]{3,2,1,0:T(8,128)S(1)}, f32[1,4,16,128]{3,2,1,0:T(8,128)}, u32[]{:S(2)}) copy-start(f32[1,4,16,128]{3,2,1,0:T(8,128)} %param.13) | copy-start | bytes 98308
  5.2 0.8 %copy-start.11 = (f32[1,4,16,128]{3,2,1,0:T(8,128)S(1)}, f32[1,4,16,128]{3,2,1,0:T(8,128)}, u32[]{:S(2)}) copy-start(f32[1,4,16,128]{3,2,1,0:T(8,128)} %param.14) | copy-start | bytes 98308
  6.0 0.8 %copy-start.12 = (f32[1,4,16,128]{3,2,1,0:T(8,128)S(1)}, f32[1,4,16,128]{3,2,1,0:T(8,128)}, u32[]{:S(2)}) copy-start(f32[1,4,16,128]{3,2,1,0:T(8,128)} %param.15) | copy-start | bytes 98308
  6.7 14.0 %collective-permute-start.2 = (f32[26,16,128]{2,1,0:T(8,128)S(1)}, f32[26,16,128]{2,1,0:T(8,128)S(1)}, u32[]{:S(2)}, u32[]{:S(2)}) collective-permute-start(f32[26,16,128]{2,1,0:T(8,128)S(1)} %constant_dynamic-update-slice_fusion.5.refs_0_), channel_id=1, source_target_pairs={{0,8},{4,12},{8,0},{12,4},{1,9},{5,13},{9,1},{13,5},{2,10},{6,14},... | collective-permute-start | bytes 638984 | tf_op jit(solution)/shard_map/ppermute | solution.py:35
  10.8 12.0 %collective-permute-start.1 = (f32[26,16,128]{2,1,0:T(8,128)S(1)}, f32[26,16,128]{2,1,0:T(8,128)S(1)}, u32[]{:S(2)}, u32[]{:S(2)}) collective-permute-start(f32[26,16,128]{2,1,0:T(8,128)S(1)} %constant_dynamic-update-slice_fusion.5.refs_0_), channel_id=1, source_target_pairs={{0,4},{4,0},{8,12},{12,8},{1,5},{5,1},{9,13},{13,9},{2,6},{6,2},{1... | collective-permute-start | bytes 638984 | tf_op jit(solution)/shard_map/ppermute | solution.py:35
  12.4 11.0 %collective-permute-start = (f32[26,16,128]{2,1,0:T(8,128)S(1)}, f32[26,16,128]{2,1,0:T(8,128)S(1)}, u32[]{:S(2)}, u32[]{:S(2)}) collective-permute-start(f32[26,16,128]{2,1,0:T(8,128)S(1)} %constant_dynamic-update-slice_fusion.5.refs_0_), channel_id=1, source_target_pairs={{0,2},{2,0},{1,3},{3,1},{4,6},{6,4},{5,7},{7,5},{8,10},{10,8},{9,1... | collective-permute-start | bytes 638984 | tf_op jit(solution)/shard_map/ppermute | solution.py:35
  20.8 12.8 %collective-permute-start.5 = (f32[26,16,128]{2,1,0:T(8,128)S(1)}, f32[26,16,128]{2,1,0:T(8,128)S(1)}, u32[]{:S(2)}, u32[]{:S(2)}) collective-permute-start(f32[26,16,128]{2,1,0:T(8,128)S(1)} %collective-permute-done.2.refs_3_), channel_id=1, source_target_pairs={{0,2},{2,0},{1,3},{3,1},{4,6},{6,4},{5,7},{7,5},{8,10},{10,8},{9,1... | collective-permute-start | bytes 638984 | tf_op jit(solution)/shard_map/ppermute | solution.py:35
  22.3 5.8 %collective-permute-start.3 = (f32[26,16,128]{2,1,0:T(8,128)S(1)}, f32[26,16,128]{2,1,0:T(8,128)S(1)}, u32[]{:S(2)}, u32[]{:S(2)}) collective-permute-start(f32[26,16,128]{2,1,0:T(8,128)S(1)} %collective-permute-done.2.refs_3_), channel_id=1, source_target_pairs={{0,4},{4,0},{8,12},{12,8},{1,5},{5,1},{9,13},{13,9},{2,6},{6,2},{1... | collective-permute-start | bytes 638984 | tf_op jit(solution)/shard_map/ppermute | solution.py:35
  22.9 10.6 %collective-permute-start.4 = (f32[26,16,128]{2,1,0:T(8,128)S(1)}, f32[26,16,128]{2,1,0:T(8,128)S(1)}, u32[]{:S(2)}, u32[]{:S(2)}) collective-permute-start(f32[26,16,128]{2,1,0:T(8,128)S(1)} %collective-permute-done.1.refs_2_), channel_id=1, source_target_pairs={{0,2},{2,0},{1,3},{3,1},{4,6},{6,4},{5,7},{7,5},{8,10},{10,8},{9,1... | collective-permute-start | bytes 638984 | tf_op jit(solution)/shard_map/ppermute | solution.py:35
  28.2 8.1 %collective-permute-start.6 = (f32[26,16,128]{2,1,0:T(8,128)S(1)}, f32[26,16,128]{2,1,0:T(8,128)S(1)}, u32[]{:S(2)}, u32[]{:S(2)}) collective-permute-start(f32[26,16,128]{2,1,0:T(8,128)S(1)} %collective-permute-done.3.refs_4_), channel_id=1, source_target_pairs={{0,2},{2,0},{1,3},{3,1},{4,6},{6,4},{5,7},{7,5},{8,10},{10,8},{9,1... | collective-permute-start | bytes 638984 | tf_op jit(solution)/shard_map/ppermute | solution.py:35
  33.6 4.9 %copy-start.1 = (bf16[256,256]{1,0:T(8,128)(2,1)S(1)}, bf16[256,256]{1,0:T(8,128)(2,1)}, u32[]{:S(2)}) copy-start(bf16[256,256]{1,0:T(8,128)(2,1)} %constant.19.clone.matrix_ref) | copy-start | bytes 393220
  36.3 2.2 %collective-permute-start.7 = (f32[8,10,16,128]{3,2,1,0:T(8,128)S(1)}, f32[8,10,16,128]{3,2,1,0:T(8,128)S(1)}, u32[]{:S(2)}, u32[]{:S(2)}) collective-permute-start(f32[8,10,16,128]{3,2,1,0:T(8,128)S(1)} %fusion), channel_id=1, source_target_pairs={{0,1},{1,0},{2,3},{3,2},{4,5},{5,4},{6,7},{7,6},{8,9},{9,8},{10,11... | collective-permute-start | bytes 1966088 | tf_op jit(solution)/shard_map/ppermute | solution.py:35
  36.4 2.1 %copy-start.3 = (s32[4]{0:T(128)S(1)}, s32[4]{0:T(128)}, u32[]{:S(2)}) copy-start(s32[4]{0:T(128)} %plan_ref.1) | copy-start | bytes 52
  36.5 26.3 %copy-start.2 = (s32[3]{0:T(128)}, s32[3]{0:T(128)S(1)}, u32[]{:S(2)}) copy-start(s32[3]{0:T(128)S(1)} %pad_add_fusion.place_ref) | copy-start | bytes 40
  62.7 1.7 %copy-start = (f32[4,12,16,128]{3,2,1,0:T(8,128)}, f32[4,12,16,128]{3,2,1,0:T(8,128)S(1)}, u32[]{:S(2)}) copy-start(f32[4,12,16,128]{3,2,1,0:T(8,128)S(1)} %get-tuple-element.8.own_ref) | copy-start | bytes 1179652
  62.7 1.7 %collective-permute-start.8 = (f32[4,12,16,128]{3,2,1,0:T(8,128)S(1)}, f32[4,12,16,128]{3,2,1,0:T(8,128)S(1)}, u32[]{:S(2)}, u32[]{:S(2)}) collective-permute-start(f32[4,12,16,128]{3,2,1,0:T(8,128)S(1)} %get-tuple-element.8.own_ref), channel_id=1, source_target_pairs={{0,1},{1,0},{2,3},{3,2},{4,5},{5,4},{6,7},{7,6},{8,9},{9,8},{10,11... | collective-permute-start | bytes 1179656 | tf_op jit(solution)/shard_map/ppermute | solution.py:35
  64.5 0.8 %copy-start.4 = (f32[4,12,16,128]{3,2,1,0:T(8,128)}, f32[4,12,16,128]{3,2,1,0:T(8,128)S(1)}, u32[]{:S(2)}) copy-start(f32[4,12,16,128]{3,2,1,0:T(8,128)S(1)} %collective-permute-done.8.other_ref) | copy-start | bytes 1179652
where the time goes:
time: 67.8 us; the launch traced here: 67.2 us
  Pallas kernels  26.2 us (39%)
  waiting for transfers between devices  22.5 us (33%)
  starting transfers between devices  10.7 us (16%)
  local copies, waits for them, and re-layouts  6.91 us (10%)
  between operations  0.74 us (1%)
    pallas_call x1, Pallas kernels, gathered_solution(): pl.pallas_call(functools.partial(steps_kernel, sizes), out_shape=(jax.Sha...  24.3 us
    ppermute x9, waiting for transfers between devices, swapped(): return lax.ppermute(block, axis, [(i, i ^ bit) for i in range(count)])  22.5 us
    ppermute x9, starting transfers between devices, swapped(): return lax.ppermute(block, axis, [(i, i ^ bit) for i in range(count)])  10.7 us
    unnamed x41, local copies, waits for them, and re-layouts  6.88 us
    pallas_call x1, Pallas kernels, gathered_solution(): pl.pallas_call(image_kernel, out_shape=jax.ShapeDtypeStruct((lags.shape[0...  1.93 us
  transfers between devices with their start and end apart: 9, of which 6 were waited for; matrix products, arithmetic and copies ran while one was open for 0% of the time, Pallas kernels for 0%

commit v1 on v0

--- a/solution.py
+++ b/solution.py
@@ -1,4 +1,5 @@
 import functools
+import math
 
 import jax
 import jax.numpy as jnp
@@ -11,6 +12,7 @@
 STEPS = 8
 REACH = 4
 ROWS = 8
+UNROLL = 4
 
 SECOND = (-205.0 / 72.0, 8.0 / 5.0, -1.0 / 5.0, 8.0 / 315.0, -1.0 / 560.0)
 FIRST = (4.0 / 5.0, -1.0 / 5.0, 4.0 / 105.0, -1.0 / 280.0)
@@ -28,6 +30,20 @@
         first += FIRST_SCALE * FIRST[m - 1] * (np.eye(depth, k=-m) - np.eye(depth, k=m))
     both = np.concatenate([second, first], axis=1)
     return jnp.asarray(np.concatenate([both, both], axis=0), jnp.bfloat16)
+
+
+def sine_cosine(angle):
+    half = 0.5 * angle
+    square = half * half
+
+    def series(first, count):
+        value = jnp.full_like(square, (-1) ** (count - 1) / math.factorial(2 * count - 2 + first))
+        for k in range(count - 2, -1, -1):
+            value = value * square + (-1) ** k / math.factorial(2 * k + first)
+        return value
+
+    sine = half * series(1, 7)
+    return 2.0 * sine * series(0, 8), 1.0 - 2.0 * sine * sine
 
 
 def swapped(block, axis, bit):
@@ -60,23 +76,40 @@
     return total
 
 
-def steps_kernel(sizes, plan_ref, place_ref, matrix_ref, *refs):
+def pack_kernel(*refs):
+    waves, earth, out_ref, sems = refs[:4], refs[4:9], refs[9], refs[10]
+    tile_x = waves[0].shape[1]
+    half = tile_x // 2
+    first = lax.axis_index("sec") * half
+    copies = []
+    for number, ref in enumerate(waves):
+        copies.append((ref.at[0], out_ref.at[pl.ds(number * tile_x, tile_x)]))
+    for number, ref in enumerate(earth):
+        copies.append((ref.at[pl.ds(first, half)], out_ref.at[pl.ds(4 * tile_x + number * half, half)]))
+    copies = [pltpu.make_async_copy(a, b, sems.at[i]) for i, (a, b) in enumerate(copies)]
+    for copy in copies:
+        copy.start()
+    for copy in copies:
+        copy.wait()
+
+
+def steps_kernel(sizes, plan_ref, matrix_ref, *refs):
     tile_x, tile_y, total_x, total_y, depth, slots, nsnap = sizes
     tiles = refs[: len(slots)]
     halves = refs[len(slots)]
     p_out, q_out, snap_out = refs[len(slots) + 1 : len(slots) + 4]
-    pa, pb, qa, qb, first_z, second_z, slope_x, weights = refs[len(slots) + 4 :]
-    gx, gy, sec = place_ref[0], place_ref[1], place_ref[2]
+    pa, pb, qa, qb, first_a, first_b, second_a, second_b, slope_x, weights = refs[len(slots) + 4 :]
+    gx, gy, sec = lax.axis_index("gx"), lax.axis_index("gy"), lax.axis_index("sec")
     half = tile_x // 2
 
     full_y = total_y + 2 * ROWS
-    for ref in (pa, pb, qa, qb, first_z.at[0], first_z.at[1]):
+    for ref in (pa, pb, qa, qb, first_a.at[0], first_a.at[1], first_b.at[0], first_b.at[1]):
         for start in (0, total_x + REACH):
             ref[start : start + REACH] = jnp.zeros((REACH, full_y, depth), jnp.float32)
         for start in (0, total_y + ROWS):
             ref[:, start : start + ROWS] = jnp.zeros((total_x + 2 * REACH, ROWS, depth), jnp.float32)
     for start in (0, total_y + ROWS):
-        slope_x[:, start : start + ROWS] = jnp.zeros((2, ROWS, depth), jnp.float32)
+        slope_x[:, start : start + ROWS] = jnp.zeros((2 * UNROLL, ROWS, depth), jnp.float32)
 
     for slot, (kx, ky) in enumerate(slots):
         ix, iy = jnp.bitwise_xor(gx, kx), jnp.bitwise_xor(gy, ky)
@@ -91,8 +124,8 @@
             base = xs + half * (jnp.bitwise_xor(sec, side))
             for row in range(half):
                 courant, epsilon, delta, tilt, azimuth = (source[g * half + row] for g in range(5))
-                sin_t, cos_t = jnp.sin(tilt), jnp.cos(tilt)
-                sin_a, cos_a = jnp.sin(azimuth), jnp.cos(azimuth)
+                sin_t, cos_t = sine_cosine(tilt)
+                sin_a, cos_a = sine_cosine(azimuth)
                 axis_x, axis_y = sin_t * cos_a, sin_t * sin_a
                 cross = courant * (2.0 * FIRST[0] / FIRST_SCALE)
                 fields = (
@@ -110,7 +143,30 @@
                     weights[number, base + row, pl.ds(ys, tile_y)] = field
 
     matrix = matrix_ref[...]
+
+    def depth_rows(x, count, fields, first_z, second_z):
+        size = count * total_y
+        parts = [ref[pl.ds(x + REACH, count), ROWS : ROWS + total_y].reshape(size, depth) for ref in fields]
+        both = jnp.concatenate(parts, axis=0)
+        high = both.astype(jnp.bfloat16)
+        low = (both - high.astype(jnp.float32)).astype(jnp.bfloat16)
+        out = jnp.dot(jnp.concatenate([high, low], axis=1), matrix, preferred_element_type=jnp.float32)
+        for f in (0, 1):
+            piece = out[f * size : (f + 1) * size]
+            second_z[f, pl.ds(x + REACH, count)] = piece[:, :depth].reshape(count, total_y, depth)
+            first_z[f, pl.ds(x + REACH, count), ROWS : ROWS + total_y] = piece[:, depth:].reshape(
+                count, total_y, depth
+            )
+
     now, before = (pa, qa), (pb, qb)
+    along_z, along_z_next = (first_a, second_a), (first_b, second_b)
+
+    def start_body(block, carry):
+        depth_rows(block * REACH, REACH, (pa, qa), first_a, second_a)
+        return carry
+
+    lax.fori_loop(0, total_x // REACH, start_body, 0)
+
     for step in range(1, STEPS + 1):
         left = REACH * (STEPS - step)
         x_low = jnp.maximum(gx * tile_x - left - REACH, 0)
@@ -120,39 +176,18 @@
             y_low = 0
         slope_length = min(y_length + 2 * ROWS, total_y)
         slope_low = 0 if slope_length == total_y else jnp.clip(y_low - ROWS, 0, total_y - slope_length)
-        z_low = jnp.maximum(x_low - REACH, 0) // REACH
-        z_high = jnp.minimum(x_high + REACH, total_x) // REACH
-
-        def depth_body(block, carry, now=now):
-            x = block * REACH
-            rows = REACH * total_y
-            parts = [
-                ref[pl.ds(x + REACH, REACH), ROWS : ROWS + total_y].reshape(rows, depth) for ref in now
-            ]
-            both = jnp.concatenate(parts, axis=0)
-            high = both.astype(jnp.bfloat16)
-            low = (both - high.astype(jnp.float32)).astype(jnp.bfloat16)
-            out = jnp.dot(
-                jnp.concatenate([high, low], axis=1), matrix, preferred_element_type=jnp.float32
-            )
-            for f in (0, 1):
-                piece = out[f * rows : (f + 1) * rows]
-                second_z[f, pl.ds(x, REACH)] = piece[:, :depth].reshape(REACH, total_y, depth)
-                first_z[f, pl.ds(x + REACH, REACH), ROWS : ROWS + total_y] = piece[:, depth:].reshape(
-                    REACH, total_y, depth
-                )
-            return carry
-
-        lax.fori_loop(z_low, z_high, depth_body, 0)
-
-        def row_body(x, carry, now=now, before=before, y_low=y_low, y_length=y_length,
-                     slope_low=slope_low, slope_length=slope_length):
+        first_z, second_z = along_z
+
+        def one_row(x, lane, now, before, y_low, y_length, slope_low, slope_length, first_z, second_z):
             row = x + REACH
+            kept = {}
             for f in (0, 1):
                 for j in range(0, slope_length, ROWS):
                     ys = pl.ds(ROWS + slope_low + j, ROWS)
-                    load = lambda m: now[f][row + m, ys]
-                    slope_x[f, ys] = pair_differences(load, FIRST_TAIL)
+                    near = {m: now[f][row + m, ys] for m in range(-REACH, REACH + 1) if m}
+                    slope_x[2 * lane + f, ys] = pair_differences(near.get, FIRST_TAIL)
+                    if y_length == total_y:
+                        kept[f, j] = pair_sums(near.get, SECOND_TAIL)
             for j in range(0, y_length, ROWS):
                 at = y_low + j
                 ys = pl.ds(at, ROWS)
@@ -160,12 +195,15 @@
                 w = [weights[i, x, ys] for i in range(9)]
                 axial = []
                 for f in (0, 1):
-                    along_x = lambda m: now[f][row + m, pl.ds(here, ROWS)]
-                    along_y = lambda m: now[f][row, pl.ds(here + m, ROWS)]
-                    curve_xx = pair_sums(along_x, SECOND_TAIL)
-                    curve_yy = pair_sums(along_y, SECOND_TAIL)
-                    curve_zz = second_z[f, x, ys]
-                    curve_xy = pair_differences(lambda m: slope_x[f, pl.ds(here + m, ROWS)], FIRST_TAIL)
+                    if (f, j) in kept:
+                        curve_xx = kept[f, j]
+                    else:
+                        curve_xx = pair_sums(lambda m: now[f][row + m, pl.ds(here, ROWS)], SECOND_TAIL)
+                    curve_yy = pair_sums(lambda m: now[f][row, pl.ds(here + m, ROWS)], SECOND_TAIL)
+                    curve_zz = second_z[f, row, ys]
+                    curve_xy = pair_differences(
+                        lambda m: slope_x[2 * lane + f, pl.ds(here + m, ROWS)], FIRST_TAIL
+                    )
                     curve_yz = pair_differences(
                         lambda m: first_z[f, row, pl.ds(here + m, ROWS)], FIRST_TAIL
                     )
@@ -185,10 +223,21 @@
                 spot = (row, pl.ds(here, ROWS))
                 before[0][spot] = 2.0 * p - before[0][spot] + w[7] * flat + shared
                 before[1][spot] = 2.0 * q - before[1][spot] + w[8] * flat + shared
+
+        def rows_body(block, carry, step=step, now=now, before=before, y_low=y_low, y_length=y_length,
+                      slope_low=slope_low, slope_length=slope_length, along_z=along_z, ahead=along_z_next):
+            x = block * UNROLL
+            if step < STEPS:
+                depth_rows(x - UNROLL, UNROLL, before, *ahead)
+            for lane in range(UNROLL):
+                one_row(x + lane, lane, now, before, y_low, y_length, slope_low, slope_length, *along_z)
             return carry
 
-        lax.fori_loop(x_low, x_high, row_body, 0)
+        lax.fori_loop(x_low // UNROLL, x_high // UNROLL, rows_body, 0)
+        if step < STEPS:
+            depth_rows(x_high - UNROLL, UNROLL, before, *along_z_next)
         now, before = before, now
+        along_z, along_z_next = along_z_next, along_z
 
         mine = pl.ds(pl.multiple_of(ROWS + gy * tile_y, ROWS), tile_y)
         for j in range(nsnap):
@@ -200,8 +249,8 @@
     q_out[0] = now[1][pl.ds(gx * tile_x + REACH, tile_x), mine]
 
 
-def image_kernel(lags_ref, place_ref, own_ref, other_ref, image_ref):
-    sec = place_ref[2]
+def image_kernel(lags_ref, own_ref, other_ref, image_ref):
+    sec = lax.axis_index("sec")
     sign = 1 - 2 * sec
     nlag, tile_x, tile_y, half = image_ref.shape
     nsnap = own_ref.shape[0]
@@ -217,16 +266,22 @@
 
 def gathered_solution(pressure, pressure_before, quasi, quasi_before, courant, epsilon, delta, tilt, azimuth, plan, lags):
     count_x, count_y = lax.axis_size("gx"), lax.axis_size("gy")
-    gx, gy, sec = lax.axis_index("gx"), lax.axis_index("gy"), lax.axis_index("sec")
     _, tile_x, tile_y, depth = pressure.shape
     total_x, total_y = count_x * tile_x, count_y * tile_y
     half = tile_x // 2
-    place = jnp.stack([gx, gy, sec]).astype(jnp.int32)
-
-    waves = jnp.concatenate([pressure[0], pressure_before[0], quasi[0], quasi_before[0]])
-    earth = jnp.stack([courant, epsilon, delta, tilt, azimuth])
-    earth = lax.dynamic_slice_in_dim(earth, sec * half, half, 1).reshape(5 * half, tile_y, depth)
-    held = {(0, 0): jnp.concatenate([waves, earth])}
+    vmem = pl.BlockSpec(memory_space=pltpu.VMEM)
+    smem = pl.BlockSpec(memory_space=pltpu.SMEM)
+    apart = pl.BlockSpec(memory_space=pl.ANY)
+
+    parts = (pressure, pressure_before, quasi, quasi_before, courant, epsilon, delta, tilt, azimuth)
+    packed = pl.pallas_call(
+        pack_kernel,
+        out_shape=jax.ShapeDtypeStruct((4 * tile_x + 5 * half, tile_y, depth), jnp.float32),
+        in_specs=[apart] * len(parts),
+        out_specs=vmem,
+        scratch_shapes=[pltpu.SemaphoreType.DMA((len(parts),))],
+    )(*parts)
+    held = {(0, 0): packed}
     for ky in range(count_y):
         if ky:
             low = ky & -ky
@@ -245,9 +300,9 @@
 
     nsnap = plan.shape[0]
     sizes = (tile_x, tile_y, total_x, total_y, depth, slots, nsnap)
-    vmem = pl.BlockSpec(memory_space=pltpu.VMEM)
-    smem = pl.BlockSpec(memory_space=pltpu.SMEM)
     field = pltpu.VMEM((total_x + 2 * REACH, total_y + 2 * ROWS, depth), jnp.float32)
+    slope = pltpu.VMEM((2, total_x + 2 * REACH, total_y + 2 * ROWS, depth), jnp.float32)
+    curve = pltpu.VMEM((2, total_x + 2 * REACH, total_y, depth), jnp.float32)
     p_final, q_final, snaps = pl.pallas_call(
         functools.partial(steps_kernel, sizes),
         out_shape=(
@@ -255,25 +310,24 @@
             jax.ShapeDtypeStruct(quasi.shape, jnp.float32),
             jax.ShapeDtypeStruct((nsnap, tile_x + 2 * REACH, tile_y, depth), jnp.float32),
         ),
-        in_specs=[smem, smem, vmem] + [vmem] * (len(tiles) + 1),
+        in_specs=[smem, vmem] + [vmem] * (len(tiles) + 1),
         out_specs=(vmem, vmem, vmem),
         scratch_shapes=[
             field, field, field, field,
-            pltpu.VMEM((2, total_x + 2 * REACH, total_y + 2 * ROWS, depth), jnp.float32),
-            pltpu.VMEM((2, total_x, total_y, depth), jnp.float32),
-            pltpu.VMEM((2, total_y + 2 * ROWS, depth), jnp.float32),
+            slope, slope, curve, curve,
+            pltpu.VMEM((2 * UNROLL, total_y + 2 * ROWS, depth), jnp.float32),
             pltpu.VMEM((9, total_x, total_y, depth), jnp.float32),
         ],
         compiler_params=pltpu.CompilerParams(vmem_limit_bytes=40 * 1024 * 1024),
-    )(plan, place, depth_matrix(depth), *tiles, other)
+    )(plan, depth_matrix(depth), *tiles, other)
 
     other_snaps = swapped(snaps, "sec", 1)
     image = pl.pallas_call(
         image_kernel,
         out_shape=jax.ShapeDtypeStruct((lags.shape[0], tile_x, tile_y, depth // 2), jnp.float32),
-        in_specs=[smem, smem, vmem, vmem],
+        in_specs=[smem, vmem, vmem],
         out_specs=vmem,
-    )(lags, place, snaps, other_snaps)
+    )(lags, snaps, other_snaps)
     return (p_final, q_final, image)
 
 

time: 67.8 us -> 57.8 us (0.85)
  local copies, waits for them, and re-layouts: 6.91 us -> 1.76 us
  Pallas kernels: 26.2 us -> 22.5 us
  waiting for transfers between devices: 22.5 us -> 21.7 us
    pallas_call x1, Pallas kernels: 24.3 us -> 18.9 us  [gathered_solution(): pl.pallas_call(functools.partial(steps_kernel, sizes), out_shape=(jax.Sha...]
    unnamed x41 -> x17, local copies, waits for them, and re-layouts: 6.88 us -> 1.75 us
    pallas_call x0 -> x1, Pallas kernels: none -> 1.61 us  [gathered_solution(): pl.pallas_call(pack_kernel, out_shape=jax.ShapeDtypeStruct((4 * tile_x +...]
    ppermute x9, waiting for transfers between devices: 22.5 us -> 21.7 us  [swapped(): return lax.ppermute(block, axis, [(i, i ^ bit) for i in range(count)])]
  transfers between devices with their start and end apart: 9 -> 9, of which waited for: 6 -> 6; matrix products, arithmetic and copies ran while one was open for 0% -> 2% of each run, Pallas kernels for 0% -> 0%
where the time goes in v1:
time: 57.8 us; the launch traced here: 57.5 us
  Pallas kernels  22.5 us (39%)
  waiting for transfers between devices  21.7 us (38%)
  starting transfers between devices  10.8 us (19%)
  local copies, waits for them, and re-layouts  1.76 us (3%)
  between operations  0.72 us (1%)
    ppermute x9, waiting for transfers between devices, swapped(): return lax.ppermute(block, axis, [(i, i ^ bit) for i in range(count)])  21.7 us
    pallas_call x1, Pallas kernels, gathered_solution(): pl.pallas_call(functools.partial(steps_kernel, sizes), out_shape=(jax.Sha...  18.9 us
    ppermute x9, starting transfers between devices, swapped(): return lax.ppermute(block, axis, [(i, i ^ bit) for i in range(count)])  10.8 us
    pallas_call x1, Pallas kernels, gathered_solution(): pl.pallas_call(image_kernel, out_shape=jax.ShapeDtypeStruct((lags.shape[0...  1.93 us
    unnamed x17, local copies, waits for them, and re-layouts  1.75 us
    pallas_call x1, Pallas kernels, gathered_solution(): pl.pallas_call(pack_kernel, out_shape=jax.ShapeDtypeStruct((4 * tile_x +...  1.61 us
  transfers between devices with their start and end apart: 9, of which 6 were waited for; matrix products, arithmetic and copies ran while one was open for 2% of the time, Pallas kernels for 0%

profile of v1, /device:TPU:0, one launch (start us, length us, event | category | flops | bytes accessed | tf_op | source)
XLA Modules:
  0.0 57.5 jit_solution(879013698301967789)
XLA Ops:
  0.6 1.6 %shard_map.139.refs_0_ = f32[26,16,128]{2,1,0:T(8,128)} custom-call(f32[1,4,16,128]{3,2,1,0:T(8,128)} %refs_0_.1, f32[1,4,16,128]{3,2,1,0:T(8,128)} %refs_1_.1, f32[1,4,16,128]{3,2,1,0:T(8,128)} %refs_2_.1, f32[1,4,16,128]{3,2,1,0:T(8,128)} %refs_3_.1, f32[4,16,128]{2,1,0:T(8,128)} %refs_4_.1, f32[4,16,128]{2,1,0:T(8,128)} %refs_5_.1, ...), custom_call_target="tpu_custom_call" | custom-call | tf_op jit(solution)/shard_map/pallas_call | solution.py:277
  2.3 4.1 %collective-permute-start.2 = (f32[26,16,128]{2,1,0:T(8,128)}, f32[26,16,128]{2,1,0:T(8,128)S(1)}, u32[]{:S(2)}, u32[]{:S(2)}) collective-permute-start(f32[26,16,128]{2,1,0:T(8,128)} %shard_map.139.refs_0_), channel_id=1, source_target_pairs={{0,8},{4,12},{8,0},{12,4},{1,9},{5,13},{9,1},{13,5},{2,10},{6,14},... | collective-permute-start | bytes 638984 | tf_op jit(solution)/shard_map/ppermute | solution.py:51
  6.4 1.6 %collective-permute-start.1 = (f32[26,16,128]{2,1,0:T(8,128)}, f32[26,16,128]{2,1,0:T(8,128)S(1)}, u32[]{:S(2)}, u32[]{:S(2)}) collective-permute-start(f32[26,16,128]{2,1,0:T(8,128)} %shard_map.139.refs_0_), channel_id=1, source_target_pairs={{0,4},{4,0},{8,12},{12,8},{1,5},{5,1},{9,13},{13,9},{2,6},{6,2},{1... | collective-permute-start | bytes 638984 | tf_op jit(solution)/shard_map/ppermute | solution.py:51
  7.9 1.5 %collective-permute-start = (f32[26,16,128]{2,1,0:T(8,128)}, f32[26,16,128]{2,1,0:T(8,128)S(1)}, u32[]{:S(2)}, u32[]{:S(2)}) collective-permute-start(f32[26,16,128]{2,1,0:T(8,128)} %shard_map.139.refs_0_), channel_id=1, source_target_pairs={{0,2},{2,0},{1,3},{3,1},{4,6},{6,4},{5,7},{7,5},{8,10},{10,8},{9,1... | collective-permute-start | bytes 638984 | tf_op jit(solution)/shard_map/ppermute | solution.py:51
  9.4 0.9 %fusion.7 = f32[8,10,16,128]{3,2,1,0:T(8,128)S(1)} fusion(f32[26,16,128]{2,1,0:T(8,128)} %shard_map.139.refs_0_), kind=kLoop, calls=%fused_computation.15 | loop fusion | bytes 163840
  10.4 6.1 %collective-permute-done.2.refs_3_ = f32[26,16,128]{2,1,0:T(8,128)S(1)} collective-permute-done((f32[26,16,128]{2,1,0:T(8,128)}, f32[26,16,128]{2,1,0:T(8,128)S(1)}, u32[]{:S(2)}, u32[]{:S(2)}) %collective-permute-start.2) | collective-permute-done | bytes 213024 | tf_op jit(solution)/shard_map/ppermute | solution.py:51
  16.5 1.5 %collective-permute-start.5 = (f32[26,16,128]{2,1,0:T(8,128)S(1)}, f32[26,16,128]{2,1,0:T(8,128)S(1)}, u32[]{:S(2)}, u32[]{:S(2)}) collective-permute-start(f32[26,16,128]{2,1,0:T(8,128)S(1)} %collective-permute-done.2.refs_3_), channel_id=1, source_target_pairs={{0,2},{2,0},{1,3},{3,1},{4,6},{6,4},{5,7},{7,5},{8,10},{10,8},{9,1... | collective-permute-start | bytes 638984 | tf_op jit(solution)/shard_map/ppermute | solution.py:51
  18.0 0.7 %collective-permute-start.3 = (f32[26,16,128]{2,1,0:T(8,128)S(1)}, f32[26,16,128]{2,1,0:T(8,128)S(1)}, u32[]{:S(2)}, u32[]{:S(2)}) collective-permute-start(f32[26,16,128]{2,1,0:T(8,128)S(1)} %collective-permute-done.2.refs_3_), channel_id=1, source_target_pairs={{0,4},{4,0},{8,12},{12,8},{1,5},{5,1},{9,13},{13,9},{2,6},{6,2},{1... | collective-permute-start | bytes 638984 | tf_op jit(solution)/shard_map/ppermute | solution.py:51
  18.7 0.0 collective-permute-done.1.refs_2_
  18.7 0.5 collective-permute-start.4
  19.2 0.0 collective-permute-done.refs_1_
  19.3 4.6 %collective-permute-done.3.refs_4_ = f32[26,16,128]{2,1,0:T(8,128)S(1)} collective-permute-done((f32[26,16,128]{2,1,0:T(8,128)S(1)}, f32[26,16,128]{2,1,0:T(8,128)S(1)}, u32[]{:S(2)}, u32[]{:S(2)}) %collective-permute-start.3) | collective-permute-done | bytes 213024 | tf_op jit(solution)/shard_map/ppermute | solution.py:51
  23.9 0.7 %collective-permute-start.6 = (f32[26,16,128]{2,1,0:T(8,128)S(1)}, f32[26,16,128]{2,1,0:T(8,128)S(1)}, u32[]{:S(2)}, u32[]{:S(2)}) collective-permute-start(f32[26,16,128]{2,1,0:T(8,128)S(1)} %collective-permute-done.3.refs_4_), channel_id=1, source_target_pairs={{0,2},{2,0},{1,3},{3,1},{4,6},{6,4},{5,7},{7,5},{8,10},{10,8},{9,1... | collective-permute-start | bytes 638984 | tf_op jit(solution)/shard_map/ppermute | solution.py:51
  24.6 4.6 %collective-permute-done.4.refs_5_ = f32[26,16,128]{2,1,0:T(8,128)S(1)} collective-permute-done((f32[26,16,128]{2,1,0:T(8,128)S(1)}, f32[26,16,128]{2,1,0:T(8,128)S(1)}, u32[]{:S(2)}, u32[]{:S(2)}) %collective-permute-start.4) | collective-permute-done | bytes 213024 | tf_op jit(solution)/shard_map/ppermute | solution.py:51
  29.3 0.0 collective-permute-done.5.refs_6_
  29.3 0.0 copy-start.3
  29.3 2.7 %collective-permute-done.6.refs_7_ = f32[26,16,128]{2,1,0:T(8,128)S(1)} collective-permute-done((f32[26,16,128]{2,1,0:T(8,128)S(1)}, f32[26,16,128]{2,1,0:T(8,128)S(1)}, u32[]{:S(2)}, u32[]{:S(2)}) %collective-permute-start.6) | collective-permute-done | bytes 213024 | tf_op jit(solution)/shard_map/ppermute | solution.py:51
  32.0 0.1 collective-permute-start.7
  32.1 2.1 %collective-permute-done.7.refs_8_ = f32[8,10,16,128]{3,2,1,0:T(8,128)S(1)} collective-permute-done((f32[8,10,16,128]{3,2,1,0:T(8,128)S(1)}, f32[8,10,16,128]{3,2,1,0:T(8,128)S(1)}, u32[]{:S(2)}, u32[]{:S(2)}) %collective-permute-start.7) | collective-permute-done | bytes 655392 | tf_op jit(solution)/shard_map/ppermute | solution.py:51
  34.2 18.9 %shard_map.140 = (f32[1,4,16,128]{3,2,1,0:T(8,128)}, f32[1,4,16,128]{3,2,1,0:T(8,128)}, f32[4,12,16,128]{3,2,1,0:T(8,128)S(1)}) custom-call(s32[4]{0:T(128)S(1)} %copy-done.3, bf16[256,256]{1,0:T(8,128)(2,1)S(1)} %copy-done.2, f32[26,16,128]{2,1,0:T(8,128)S(1)} %copy-done, f32[26,16,128]{2,1,0:T(8,128)S(1)} %collective-permute-done.refs_1_, ...), custom_call_target="tpu_custom_call" | custom-call | tf_op jit(solution)/shard_map/pallas_call | solution.py:306
  53.1 0.1 collective-permute-start.8
  53.2 1.6 %collective-permute-done.8.other_ref = f32[4,12,16,128]{3,2,1,0:T(8,128)S(1)} collective-permute-done((f32[4,12,16,128]{3,2,1,0:T(8,128)S(1)}, f32[4,12,16,128]{3,2,1,0:T(8,128)S(1)}, u32[]{:S(2)}, u32[]{:S(2)}) %collective-permute-start.8) | collective-permute-done | bytes 393248 | tf_op jit(solution)/shard_map/ppermute | solution.py:51
  54.8 0.8 %copy-done.4 = f32[4,12,16,128]{3,2,1,0:T(8,128)} copy-done((f32[4,12,16,128]{3,2,1,0:T(8,128)}, f32[4,12,16,128]{3,2,1,0:T(8,128)S(1)}, u32[]{:S(2)}) %copy-start.4) | copy-done | bytes 393240
  55.6 1.9 %shard_map.141 = f32[5,4,16,64]{3,2,1,0:T(8,128)} custom-call(s32[5]{0:T(128)} %lags_ref.1, f32[4,12,16,128]{3,2,1,0:T(8,128)} %copy-done.1, f32[4,12,16,128]{3,2,1,0:T(8,128)} %copy-done.4), custom_call_target="tpu_custom_call" | custom-call | tf_op jit(solution)/shard_map/pallas_call | solution.py:325
  (15 shorter events, 0.1 us)
Async XLA Ops:
  2.3 14.2 %collective-permute-start.2 = (f32[26,16,128]{2,1,0:T(8,128)}, f32[26,16,128]{2,1,0:T(8,128)S(1)}, u32[]{:S(2)}, u32[]{:S(2)}) collective-permute-start(f32[26,16,128]{2,1,0:T(8,128)} %shard_map.139.refs_0_), channel_id=1, source_target_pairs={{0,8},{4,12},{8,0},{12,4},{1,9},{5,13},{9,1},{13,5},{2,10},{6,14},... | collective-permute-start | bytes 638984 | tf_op jit(solution)/shard_map/ppermute | solution.py:51
  6.4 12.3 %collective-permute-start.1 = (f32[26,16,128]{2,1,0:T(8,128)}, f32[26,16,128]{2,1,0:T(8,128)S(1)}, u32[]{:S(2)}, u32[]{:S(2)}) collective-permute-start(f32[26,16,128]{2,1,0:T(8,128)} %shard_map.139.refs_0_), channel_id=1, source_target_pairs={{0,4},{4,0},{8,12},{12,8},{1,5},{5,1},{9,13},{13,9},{2,6},{6,2},{1... | collective-permute-start | bytes 638984 | tf_op jit(solution)/shard_map/ppermute | solution.py:51
  7.9 11.3 %collective-permute-start = (f32[26,16,128]{2,1,0:T(8,128)}, f32[26,16,128]{2,1,0:T(8,128)S(1)}, u32[]{:S(2)}, u32[]{:S(2)}) collective-permute-start(f32[26,16,128]{2,1,0:T(8,128)} %shard_map.139.refs_0_), channel_id=1, source_target_pairs={{0,2},{2,0},{1,3},{3,1},{4,6},{6,4},{5,7},{7,5},{8,10},{10,8},{9,1... | collective-permute-start | bytes 638984 | tf_op jit(solution)/shard_map/ppermute | solution.py:51
  16.5 12.8 %collective-permute-start.5 = (f32[26,16,128]{2,1,0:T(8,128)S(1)}, f32[26,16,128]{2,1,0:T(8,128)S(1)}, u32[]{:S(2)}, u32[]{:S(2)}) collective-permute-start(f32[26,16,128]{2,1,0:T(8,128)S(1)} %collective-permute-done.2.refs_3_), channel_id=1, source_target_pairs={{0,2},{2,0},{1,3},{3,1},{4,6},{6,4},{5,7},{7,5},{8,10},{10,8},{9,1... | collective-permute-start | bytes 638984 | tf_op jit(solution)/shard_map/ppermute | solution.py:51
  18.0 5.8 %collective-permute-start.3 = (f32[26,16,128]{2,1,0:T(8,128)S(1)}, f32[26,16,128]{2,1,0:T(8,128)S(1)}, u32[]{:S(2)}, u32[]{:S(2)}) collective-permute-start(f32[26,16,128]{2,1,0:T(8,128)S(1)} %collective-permute-done.2.refs_3_), channel_id=1, source_target_pairs={{0,4},{4,0},{8,12},{12,8},{1,5},{5,1},{9,13},{13,9},{2,6},{6,2},{1... | collective-permute-start | bytes 638984 | tf_op jit(solution)/shard_map/ppermute | solution.py:51
  18.7 10.5 %collective-permute-start.4 = (f32[26,16,128]{2,1,0:T(8,128)S(1)}, f32[26,16,128]{2,1,0:T(8,128)S(1)}, u32[]{:S(2)}, u32[]{:S(2)}) collective-permute-start(f32[26,16,128]{2,1,0:T(8,128)S(1)} %collective-permute-done.1.refs_2_), channel_id=1, source_target_pairs={{0,2},{2,0},{1,3},{3,1},{4,6},{6,4},{5,7},{7,5},{8,10},{10,8},{9,1... | collective-permute-start | bytes 638984 | tf_op jit(solution)/shard_map/ppermute | solution.py:51
  23.9 8.1 %collective-permute-start.6 = (f32[26,16,128]{2,1,0:T(8,128)S(1)}, f32[26,16,128]{2,1,0:T(8,128)S(1)}, u32[]{:S(2)}, u32[]{:S(2)}) collective-permute-start(f32[26,16,128]{2,1,0:T(8,128)S(1)} %collective-permute-done.3.refs_4_), channel_id=1, source_target_pairs={{0,2},{2,0},{1,3},{3,1},{4,6},{6,4},{5,7},{7,5},{8,10},{10,8},{9,1... | collective-permute-start | bytes 638984 | tf_op jit(solution)/shard_map/ppermute | solution.py:51
  24.6 9.5 %copy-start = (f32[26,16,128]{2,1,0:T(8,128)S(1)}, f32[26,16,128]{2,1,0:T(8,128)}, u32[]{:S(2)}) copy-start(f32[26,16,128]{2,1,0:T(8,128)} %shard_map.139.refs_0_) | copy-start | bytes 638980
  29.3 4.9 %copy-start.2 = (bf16[256,256]{1,0:T(8,128)(2,1)S(1)}, bf16[256,256]{1,0:T(8,128)(2,1)}, u32[]{:S(2)}) copy-start(bf16[256,256]{1,0:T(8,128)(2,1)} %constant.2.clone.matrix_ref) | copy-start | bytes 393220
  29.3 4.9 %copy-start.3 = (s32[4]{0:T(128)S(1)}, s32[4]{0:T(128)}, u32[]{:S(2)}) copy-start(s32[4]{0:T(128)} %plan_ref.1) | copy-start | bytes 52
  32.0 2.2 %collective-permute-start.7 = (f32[8,10,16,128]{3,2,1,0:T(8,128)S(1)}, f32[8,10,16,128]{3,2,1,0:T(8,128)S(1)}, u32[]{:S(2)}, u32[]{:S(2)}) collective-permute-start(f32[8,10,16,128]{3,2,1,0:T(8,128)S(1)} %fusion), channel_id=1, source_target_pairs={{0,1},{1,0},{2,3},{3,2},{4,5},{5,4},{6,7},{7,6},{8,9},{9,8},{10,11... | collective-permute-start | bytes 1966088 | tf_op jit(solution)/shard_map/ppermute | solution.py:51
  53.1 1.7 %copy-start.1 = (f32[4,12,16,128]{3,2,1,0:T(8,128)}, f32[4,12,16,128]{3,2,1,0:T(8,128)S(1)}, u32[]{:S(2)}) copy-start(f32[4,12,16,128]{3,2,1,0:T(8,128)S(1)} %get-tuple-element.8.own_ref) | copy-start | bytes 1179652
  53.1 1.7 %collective-permute-start.8 = (f32[4,12,16,128]{3,2,1,0:T(8,128)S(1)}, f32[4,12,16,128]{3,2,1,0:T(8,128)S(1)}, u32[]{:S(2)}, u32[]{:S(2)}) collective-permute-start(f32[4,12,16,128]{3,2,1,0:T(8,128)S(1)} %get-tuple-element.8.own_ref), channel_id=1, source_target_pairs={{0,1},{1,0},{2,3},{3,2},{4,5},{5,4},{6,7},{7,6},{8,9},{9,8},{10,11... | collective-permute-start | bytes 1179656 | tf_op jit(solution)/shard_map/ppermute | solution.py:51
  54.8 0.8 %copy-start.4 = (f32[4,12,16,128]{3,2,1,0:T(8,128)}, f32[4,12,16,128]{3,2,1,0:T(8,128)S(1)}, u32[]{:S(2)}) copy-start(f32[4,12,16,128]{3,2,1,0:T(8,128)S(1)} %collective-permute-done.8.other_ref) | copy-start | bytes 1179652

commit v2 on v1

--- a/solution.py
+++ b/solution.py
@@ -12,7 +12,6 @@
 STEPS = 8
 REACH = 4
 ROWS = 8
-UNROLL = 4
 
 SECOND = (-205.0 / 72.0, 8.0 / 5.0, -1.0 / 5.0, 8.0 / 315.0, -1.0 / 560.0)
 FIRST = (4.0 / 5.0, -1.0 / 5.0, 4.0 / 105.0, -1.0 / 280.0)
@@ -22,14 +21,24 @@
 FIRST_SCALE = 840.0 / 1024.0
 
 
+def bands(size):
+    second = np.zeros((size, size))
+    first = np.zeros((size, size))
+    for m in range(1, REACH + 1):
+        second += SECOND_SCALE * SECOND[m] * (np.eye(size, k=m) + np.eye(size, k=-m))
+        first += FIRST_SCALE * FIRST[m - 1] * (np.eye(size, k=m) - np.eye(size, k=-m))
+    return second, first
+
+
 def depth_matrix(depth):
-    second = np.zeros((depth, depth))
-    first = np.zeros((depth, depth))
-    for m in range(1, REACH + 1):
-        second += SECOND_SCALE * SECOND[m] * (np.eye(depth, k=m) + np.eye(depth, k=-m))
-        first += FIRST_SCALE * FIRST[m - 1] * (np.eye(depth, k=-m) - np.eye(depth, k=m))
-    both = np.concatenate([second, first], axis=1)
+    second, first = bands(depth)
+    both = np.concatenate([second.T, first.T], axis=1)
     return jnp.asarray(np.concatenate([both, both], axis=0), jnp.bfloat16)
+
+
+def lateral_matrix(size):
+    rows = [np.kron(np.eye(REACH), band) for band in bands(size)]
+    return jnp.asarray(np.concatenate([np.concatenate([r, r], axis=1) for r in rows], axis=0), jnp.bfloat16)
 
 
 def sine_cosine(angle):
@@ -93,160 +102,144 @@
         copy.wait()
 
 
-def steps_kernel(sizes, plan_ref, matrix_ref, *refs):
+def split(values):
+    high = values.astype(jnp.bfloat16)
+    return high, (values - high.astype(jnp.float32)).astype(jnp.bfloat16)
+
+
+def steps_kernel(sizes, plan_ref, depth_ref, lateral_ref, *refs):
     tile_x, tile_y, total_x, total_y, depth, slots, nsnap = sizes
     tiles = refs[: len(slots)]
-    halves = refs[len(slots)]
-    p_out, q_out, snap_out = refs[len(slots) + 1 : len(slots) + 4]
-    pa, pb, qa, qb, first_a, first_b, second_a, second_b, slope_x, weights = refs[len(slots) + 4 :]
+    halves = [ref.at[i] for ref in refs[len(slots) : len(slots) + 2] for i in range(ref.shape[0])]
+    p_out, q_out, snap_out = refs[len(slots) + 2 : len(slots) + 5]
+    pa, pb, qa, qb, slope_a, slope_b, rest_a, rest_b, weights, kept = refs[len(slots) + 5 :]
     gx, gy, sec = lax.axis_index("gx"), lax.axis_index("gy"), lax.axis_index("sec")
     half = tile_x // 2
-
-    full_y = total_y + 2 * ROWS
-    for ref in (pa, pb, qa, qb, first_a.at[0], first_a.at[1], first_b.at[0], first_b.at[1]):
+    blocks = total_x // REACH
+    size = REACH * total_y
+
+    slopes = [ref.at[i, f] for ref in (slope_a, slope_b) for i in (0, 1) for f in (0, 1)]
+    for ref in (pa, pb, qa, qb, *slopes):
         for start in (0, total_x + REACH):
-            ref[start : start + REACH] = jnp.zeros((REACH, full_y, depth), jnp.float32)
-        for start in (0, total_y + ROWS):
-            ref[:, start : start + ROWS] = jnp.zeros((total_x + 2 * REACH, ROWS, depth), jnp.float32)
-    for start in (0, total_y + ROWS):
-        slope_x[:, start : start + ROWS] = jnp.zeros((2 * UNROLL, ROWS, depth), jnp.float32)
+            ref[start : start + REACH] = jnp.zeros((REACH, total_y, depth), jnp.float32)
 
     for slot, (kx, ky) in enumerate(slots):
         ix, iy = jnp.bitwise_xor(gx, kx), jnp.bitwise_xor(gy, ky)
         xs = ix * tile_x
-        ys = pl.multiple_of(iy * tile_y, ROWS)
+        ys = pl.ds(pl.multiple_of(iy * tile_y, ROWS), tile_y)
         for number, ref in enumerate((pa, pb, qa, qb)):
-            ref[pl.ds(xs + REACH, tile_x), pl.ds(pl.multiple_of(ys + ROWS, ROWS), tile_y)] = tiles[slot][
-                number * tile_x : (number + 1) * tile_x
-            ]
+            ref[pl.ds(xs + REACH, tile_x), ys] = tiles[slot][number * tile_x : (number + 1) * tile_x]
         for side in (0, 1):
-            source = halves.at[slot] if side else tiles[slot].at[4 * tile_x :]
+            source = halves[slot] if side else tiles[slot].at[4 * tile_x :]
             base = xs + half * (jnp.bitwise_xor(sec, side))
             for row in range(half):
                 courant, epsilon, delta, tilt, azimuth = (source[g * half + row] for g in range(5))
                 sin_t, cos_t = sine_cosine(tilt)
                 sin_a, cos_a = sine_cosine(azimuth)
                 axis_x, axis_y = sin_t * cos_a, sin_t * sin_a
+                near, curve = courant * SECOND[1], courant * (1.0 / SECOND_SCALE)
                 cross = courant * (2.0 * FIRST[0] / FIRST_SCALE)
+                xx, yy, zz = axis_x * axis_x, axis_y * axis_y, cos_t * cos_t
                 fields = (
-                    courant * SECOND[1] * axis_x * axis_x,
-                    courant * SECOND[1] * axis_y * axis_y,
-                    courant * (1.0 / SECOND_SCALE) * cos_t * cos_t,
-                    courant * (2.0 * FIRST[0] * FIRST[0]) * axis_x * axis_y,
-                    cross * axis_y * cos_t,
+                    near * xx,
+                    curve * yy,
+                    curve * zz,
+                    near - near * xx,
+                    curve - curve * yy,
+                    curve - curve * zz,
+                    cross * axis_x * axis_y,
+                    courant * (2.0 / (FIRST_SCALE * FIRST_SCALE)) * axis_y * cos_t,
                     cross * axis_x * cos_t,
-                    courant * SECOND[1],
+                    courant * SECOND[0],
                     1.0 + 2.0 * epsilon,
                     1.0 + 2.0 * delta,
                 )
                 for number, field in enumerate(fields):
-                    weights[number, base + row, pl.ds(ys, tile_y)] = field
-
-    matrix = matrix_ref[...]
-
-    def depth_rows(x, count, fields, first_z, second_z):
-        size = count * total_y
-        parts = [ref[pl.ds(x + REACH, count), ROWS : ROWS + total_y].reshape(size, depth) for ref in fields]
-        both = jnp.concatenate(parts, axis=0)
-        high = both.astype(jnp.bfloat16)
-        low = (both - high.astype(jnp.float32)).astype(jnp.bfloat16)
-        out = jnp.dot(jnp.concatenate([high, low], axis=1), matrix, preferred_element_type=jnp.float32)
+                    weights[number, base + row, ys] = field
+
+    def lateral(first, last, parts):
+        matrix = lateral_ref[first * size : last * size]
+        return jnp.dot(matrix, jnp.concatenate(parts, axis=0), preferred_element_type=jnp.float32)
+
+    def put(ref, number, rows, values):
         for f in (0, 1):
-            piece = out[f * size : (f + 1) * size]
-            second_z[f, pl.ds(x + REACH, count)] = piece[:, :depth].reshape(count, total_y, depth)
-            first_z[f, pl.ds(x + REACH, count), ROWS : ROWS + total_y] = piece[:, depth:].reshape(
-                count, total_y, depth
-            )
-
-    now, before = (pa, qa), (pb, qb)
-    along_z, along_z_next = (first_a, second_a), (first_b, second_b)
-
-    def start_body(block, carry):
-        depth_rows(block * REACH, REACH, (pa, qa), first_a, second_a)
-        return carry
-
-    lax.fori_loop(0, total_x // REACH, start_body, 0)
-
+            ref[number, f, rows] = values[:, f * depth : (f + 1) * depth].reshape(REACH, total_y, depth)
+
+    def prepare(block, fields, slope, rest):
+        x = block * REACH
+        inner, outer = pl.ds(x, REACH), pl.ds(x + REACH, REACH)
+        high, low = split(jnp.concatenate([ref[outer].reshape(size, depth) for ref in fields], axis=0))
+        beside = lambda v: jnp.concatenate([v[:size], v[size:]], axis=1)
+        out = jnp.dot(
+            jnp.concatenate([high, low], axis=1), depth_ref[...], preferred_element_type=jnp.float32
+        )
+        along_y = lateral(0, 2, [beside(high), beside(low)])
+        along_z = beside(out[:, depth:])
+        put(rest, 0, inner, along_y[:size])
+        put(rest, 1, inner, beside(out[:, :depth]))
+        put(slope, 0, outer, along_y[size:])
+        put(slope, 1, outer, along_z)
+        put(rest, 2, inner, lateral(1, 2, split(along_z)))
+
+    def update(block, now, before, slope, rest, y_low, y_length):
+        for lane in range(REACH):
+            x = block * REACH + lane
+            row = x + REACH
+            for j in range(0, y_length, ROWS):
+                ys = pl.ds(y_low + j, ROWS)
+                w = [weights[i, x, ys] for i in range(12)]
+                curves, shears = [], []
+                for f in (0, 1):
+                    curve_xx = pair_sums(lambda m: now[f][row + m, ys], SECOND_TAIL)
+                    curve_xy = pair_differences(lambda m: slope[0, f, row + m, ys], FIRST_TAIL)
+                    curve_xz = pair_differences(lambda m: slope[1, f, row + m, ys], FIRST_TAIL)
+                    curve_yy, curve_zz, curve_yz = (rest[i, f, x, ys] for i in range(3))
+                    u = w[3:6] if f == 0 else w[0:3]
+                    curves.append(u[0] * curve_xx + u[1] * curve_yy + u[2] * curve_zz)
+                    shears.append(w[6] * curve_xy + w[7] * curve_yz + w[8] * curve_xz)
+                p, q = now[0][row, ys], now[1][row, ys]
+                p = p + p
+                flat = curves[0] - shears[0] + w[9] * p
+                axial = curves[1] + shears[1] + w[9] * q
+                before[0][row, ys] = p - before[0][row, ys] + w[10] * flat + axial
+                before[1][row, ys] = (q + q) - before[1][row, ys] + w[11] * flat + axial
+
+    mine = pl.ds(pl.multiple_of(gy * tile_y, ROWS), tile_y)
+
+    def keep(step, field):
+        slot = nsnap
+        for j in range(nsnap):
+            slot = jnp.where(plan_ref[j] == step, j, slot)
+        kept[slot] = field[pl.ds(gx * tile_x, tile_x + 2 * REACH), mine]
+
+    even = ((pa, qa), slope_a, rest_a)
+    odd = ((pb, qb), slope_b, rest_b)
+    for block in range(blocks - 1):
+        prepare(block, *even)
+
+    now, ahead, last = even, odd, blocks - 1
     for step in range(1, STEPS + 1):
         left = REACH * (STEPS - step)
-        x_low = jnp.maximum(gx * tile_x - left - REACH, 0)
-        x_high = jnp.minimum((gx + 1) * tile_x + left + REACH, total_x)
+        x_low, x_length = window(gx, tile_x, left + REACH, total_x, REACH)
         y_low, y_length = window(gy, tile_y, left, total_y, ROWS)
-        if y_length == total_y:
-            y_low = 0
-        slope_length = min(y_length + 2 * ROWS, total_y)
-        slope_low = 0 if slope_length == total_y else jnp.clip(y_low - ROWS, 0, total_y - slope_length)
-        first_z, second_z = along_z
-
-        def one_row(x, lane, now, before, y_low, y_length, slope_low, slope_length, first_z, second_z):
-            row = x + REACH
-            kept = {}
-            for f in (0, 1):
-                for j in range(0, slope_length, ROWS):
-                    ys = pl.ds(ROWS + slope_low + j, ROWS)
-                    near = {m: now[f][row + m, ys] for m in range(-REACH, REACH + 1) if m}
-                    slope_x[2 * lane + f, ys] = pair_differences(near.get, FIRST_TAIL)
-                    if y_length == total_y:
-                        kept[f, j] = pair_sums(near.get, SECOND_TAIL)
-            for j in range(0, y_length, ROWS):
-                at = y_low + j
-                ys = pl.ds(at, ROWS)
-                here = ROWS + at
-                w = [weights[i, x, ys] for i in range(9)]
-                axial = []
-                for f in (0, 1):
-                    if (f, j) in kept:
-                        curve_xx = kept[f, j]
-                    else:
-                        curve_xx = pair_sums(lambda m: now[f][row + m, pl.ds(here, ROWS)], SECOND_TAIL)
-                    curve_yy = pair_sums(lambda m: now[f][row, pl.ds(here + m, ROWS)], SECOND_TAIL)
-                    curve_zz = second_z[f, row, ys]
-                    curve_xy = pair_differences(
-                        lambda m: slope_x[2 * lane + f, pl.ds(here + m, ROWS)], FIRST_TAIL
-                    )
-                    curve_yz = pair_differences(
-                        lambda m: first_z[f, row, pl.ds(here + m, ROWS)], FIRST_TAIL
-                    )
-                    curve_xz = pair_differences(
-                        lambda m: first_z[f, row + m, pl.ds(here, ROWS)], FIRST_TAIL
-                    )
-                    axial.append(
-                        w[0] * curve_xx + w[1] * curve_yy + w[2] * curve_zz
-                        + w[3] * curve_xy + w[4] * curve_yz + w[5] * curve_xz
-                    )
-                    if f == 0:
-                        laplace = curve_xx + curve_yy + curve_zz * (1.0 / (SECOND_SCALE * SECOND[1]))
-                p = now[0][row, pl.ds(here, ROWS)]
-                q = now[1][row, pl.ds(here, ROWS)]
-                flat = w[6] * (laplace + (2.0 * SECOND[0] / SECOND[1]) * p) - axial[0]
-                shared = axial[1] + w[6] * ((SECOND[0] / SECOND[1]) * q)
-                spot = (row, pl.ds(here, ROWS))
-                before[0][spot] = 2.0 * p - before[0][spot] + w[7] * flat + shared
-                before[1][spot] = 2.0 * q - before[1][spot] + w[8] * flat + shared
-
-        def rows_body(block, carry, step=step, now=now, before=before, y_low=y_low, y_length=y_length,
-                      slope_low=slope_low, slope_length=slope_length, along_z=along_z, ahead=along_z_next):
-            x = block * UNROLL
-            if step < STEPS:
-                depth_rows(x - UNROLL, UNROLL, before, *ahead)
-            for lane in range(UNROLL):
-                one_row(x + lane, lane, now, before, y_low, y_length, slope_low, slope_length, *along_z)
-            return carry
-
-        lax.fori_loop(x_low // UNROLL, x_high // UNROLL, rows_body, 0)
-        if step < STEPS:
-            depth_rows(x_high - UNROLL, UNROLL, before, *along_z_next)
-        now, before = before, now
-        along_z, along_z_next = along_z_next, along_z
-
-        mine = pl.ds(pl.multiple_of(ROWS + gy * tile_y, ROWS), tile_y)
-        for j in range(nsnap):
-            @pl.when(plan_ref[j] == step)
-            def _():
-                snap_out[j] = now[0][pl.ds(gx * tile_x, tile_x + 2 * REACH), mine]
-
-    p_out[0] = now[0][pl.ds(gx * tile_x + REACH, tile_x), mine]
-    q_out[0] = now[1][pl.ds(gx * tile_x + REACH, tile_x), mine]
+        first = 0 if x_length == total_x else x_low // REACH
+        y_low = 0 if y_length == total_y else pl.multiple_of(y_low, ROWS)
+        count = x_length // REACH
+        if count < 3:
+            prepare(last, *now)
+        for number in range(count):
+            update(first + number, now[0], ahead[0], now[1], now[2], y_low, y_length)
+            if number == 0 and count >= 3:
+                prepare(last, *now)
+            if number and step < STEPS:
+                prepare(first + number - 1, *ahead)
+        last = first + count - 1
+        now, ahead = ahead, now
+        keep(step, now[0][0])
+
+    snap_out[...] = kept[:nsnap]
+    p_out[0] = now[0][0][pl.ds(gx * tile_x + REACH, tile_x), mine]
+    q_out[0] = now[0][1][pl.ds(gx * tile_x + REACH, tile_x), mine]
 
 
 def image_kernel(lags_ref, own_ref, other_ref, image_ref):
@@ -290,19 +283,26 @@
         low = kx & -kx
         rest = kx ^ low
         held[kx, 0] = swapped(held[rest, 0] if rest else held[0, 0], "gx", low)
-    for kx in range(1, count_x):
-        for ky in range(1, count_y):
+    for ky in range(1, count_y):
+        for kx in range(1, count_x):
             low = ky & -ky
-            held[kx, ky] = swapped(held[kx, ky ^ low], "gy", low)
+            if kx == 1:
+                held[kx, ky] = swapped(held[0, ky], "gx", 1)
+            else:
+                held[kx, ky] = swapped(held[kx, ky ^ low], "gy", low)
     slots = tuple(held)
     tiles = list(held.values())
-    other = swapped(jnp.stack([t[4 * tile_x :] for t in tiles]), "sec", 1)
+    direct = [s for s in slots if 0 in s and all(k & (k - 1) == 0 for k in s)]
+    relayed = [s for s in slots if s not in direct]
+    slots = tuple(direct + relayed)
+    tiles = [held[s] for s in slots]
+    others = [swapped(jnp.stack([held[s][4 * tile_x :] for s in part]), "sec", 1) for part in (direct, relayed)]
 
     nsnap = plan.shape[0]
     sizes = (tile_x, tile_y, total_x, total_y, depth, slots, nsnap)
-    field = pltpu.VMEM((total_x + 2 * REACH, total_y + 2 * ROWS, depth), jnp.float32)
-    slope = pltpu.VMEM((2, total_x + 2 * REACH, total_y + 2 * ROWS, depth), jnp.float32)
-    curve = pltpu.VMEM((2, total_x + 2 * REACH, total_y, depth), jnp.float32)
+    field = pltpu.VMEM((total_x + 2 * REACH, total_y, depth), jnp.float32)
+    slope = pltpu.VMEM((2, 2, total_x + 2 * REACH, total_y, depth), jnp.float32)
+    rest = pltpu.VMEM((3, 2, total_x, total_y, depth), jnp.float32)
     p_final, q_final, snaps = pl.pallas_call(
         functools.partial(steps_kernel, sizes),
         out_shape=(
@@ -310,16 +310,16 @@
             jax.ShapeDtypeStruct(quasi.shape, jnp.float32),
             jax.ShapeDtypeStruct((nsnap, tile_x + 2 * REACH, tile_y, depth), jnp.float32),
         ),
-        in_specs=[smem, vmem] + [vmem] * (len(tiles) + 1),
+        in_specs=[smem, vmem, vmem] + [vmem] * (len(tiles) + 2),
         out_specs=(vmem, vmem, vmem),
         scratch_shapes=[
             field, field, field, field,
-            slope, slope, curve, curve,
-            pltpu.VMEM((2 * UNROLL, total_y + 2 * ROWS, depth), jnp.float32),
-            pltpu.VMEM((9, total_x, total_y, depth), jnp.float32),
+            slope, slope, rest, rest,
+            pltpu.VMEM((12, total_x, total_y, depth), jnp.float32),
+            pltpu.VMEM((nsnap + 1, tile_x + 2 * REACH, tile_y, depth), jnp.float32),
         ],
-        compiler_params=pltpu.CompilerParams(vmem_limit_bytes=40 * 1024 * 1024),
-    )(plan, depth_matrix(depth), *tiles, other)
+        compiler_params=pltpu.CompilerParams(vmem_limit_bytes=24 * 1024 * 1024),
+    )(plan, depth_matrix(depth), lateral_matrix(total_y), *tiles, *others)
 
     other_snaps = swapped(snaps, "sec", 1)
     image = pl.pallas_call(
@@ -472,7 +472,8 @@
     _, tile_x, tile_y, depth = args[0].shape
     cells = count_x * tile_x * count_y * tile_y * depth
     fits = (
-        cells <= 1 << 17
+        cells <= 1 << 16
+        and count_x * tile_x <= 8 * REACH
         and count_x & (count_x - 1) == 0
         and count_y & (count_y - 1) == 0
         and tile_x % REACH == 0

time: 57.8 us -> 48.9 us (0.85)
  Pallas kernels: 22.5 us -> 16.1 us
  waiting for transfers between devices: 21.7 us -> 16.8 us
  starting transfers between devices: 10.8 us -> 13.2 us
    pallas_call x1, Pallas kernels: 18.9 us -> 12.6 us  [gathered_solution(): pl.pallas_call(functools.partial(steps_kernel, sizes), out_shape=(jax.Sha...]
    ppermute x9 -> x10, waiting for transfers between devices: 21.7 us -> 16.8 us  [swapped(): return lax.ppermute(block, axis, [(i, i ^ bit) for i in range(count)])]
    ppermute x9 -> x10, starting transfers between devices: 10.8 us -> 13.2 us  [swapped(): return lax.ppermute(block, axis, [(i, i ^ bit) for i in range(count)])]
    unnamed x17 -> x12, local copies, waits for them, and re-layouts: 1.75 us -> 0.78 us
    another operation x1 -> x8, local copies, waits for them, and re-layouts: 0.01 us -> 0.97 us  [gathered_solution(): jnp.stack([held[s][4 * tile_x:] for s in part])]
  transfers between devices with their start and end apart: 9 -> 10, of which waited for: 6 -> 6; matrix products, arithmetic and copies ran while one was open for 2% -> 2% of each run, Pallas kernels for 0% -> 0%
where the time goes in v2:
time: 48.9 us; the launch traced here: 48.7 us
  waiting for transfers between devices  16.8 us (34%)
  Pallas kernels  16.1 us (33%)
  starting transfers between devices  13.2 us (27%)
  local copies, waits for them, and re-layouts  1.75 us (4%)
  between operations  0.77 us (2%)
    ppermute x10, waiting for transfers between devices, swapped(): return lax.ppermute(block, axis, [(i, i ^ bit) for i in range(count)])  16.8 us
    ppermute x10, starting transfers between devices, swapped(): return lax.ppermute(block, axis, [(i, i ^ bit) for i in range(count)])  13.2 us
    pallas_call x1, Pallas kernels, gathered_solution(): pl.pallas_call(functools.partial(steps_kernel, sizes), out_shape=(jax.Sha...  12.6 us
    pallas_call x1, Pallas kernels, gathered_solution(): pl.pallas_call(image_kernel, out_shape=jax.ShapeDtypeStruct((lags.shape[0...  1.93 us
    pallas_call x1, Pallas kernels, gathered_solution(): pl.pallas_call(pack_kernel, out_shape=jax.ShapeDtypeStruct((4 * tile_x +...  1.6 us
  transfers between devices with their start and end apart: 10, of which 6 were waited for; matrix products, arithmetic and copies ran while one was open for 2% of the time, Pallas kernels for 0%

profile of v2, /device:TPU:0, one launch (start us, length us, event | category | flops | bytes accessed | tf_op | source)
XLA Modules:
  0.0 48.7 jit_solution(8028216913703785823)
XLA Ops:
  0.6 1.6 %shard_map.148.refs_0_ = f32[26,16,128]{2,1,0:T(8,128)} custom-call(f32[1,4,16,128]{3,2,1,0:T(8,128)} %refs_0_.1, f32[1,4,16,128]{3,2,1,0:T(8,128)} %refs_1_.1, f32[1,4,16,128]{3,2,1,0:T(8,128)} %refs_2_.1, f32[1,4,16,128]{3,2,1,0:T(8,128)} %refs_3_.1, f32[4,16,128]{2,1,0:T(8,128)} %refs_4_.1, f32[4,16,128]{2,1,0:T(8,128)} %refs_5_.1, ...), custom_call_target="tpu_custom_call" | custom-call | tf_op jit(solution)/shard_map/pallas_call | solution.py:270
  2.2 4.1 %collective-permute-start.2 = (f32[26,16,128]{2,1,0:T(8,128)}, f32[26,16,128]{2,1,0:T(8,128)S(1)}, u32[]{:S(2)}, u32[]{:S(2)}) collective-permute-start(f32[26,16,128]{2,1,0:T(8,128)} %shard_map.148.refs_0_), channel_id=1, source_target_pairs={{0,8},{4,12},{8,0},{12,4},{1,9},{5,13},{9,1},{13,5},{2,10},{6,14},... | collective-permute-start | bytes 638984 | tf_op jit(solution)/shard_map/ppermute | solution.py:60
  6.3 1.6 %collective-permute-start.1 = (f32[26,16,128]{2,1,0:T(8,128)}, f32[26,16,128]{2,1,0:T(8,128)S(1)}, u32[]{:S(2)}, u32[]{:S(2)}) collective-permute-start(f32[26,16,128]{2,1,0:T(8,128)} %shard_map.148.refs_0_), channel_id=1, source_target_pairs={{0,4},{4,0},{8,12},{12,8},{1,5},{5,1},{9,13},{13,9},{2,6},{6,2},{1... | collective-permute-start | bytes 638984 | tf_op jit(solution)/shard_map/ppermute | solution.py:60
  7.9 1.5 %collective-permute-start = (f32[26,16,128]{2,1,0:T(8,128)}, f32[26,16,128]{2,1,0:T(8,128)S(1)}, u32[]{:S(2)}, u32[]{:S(2)}) collective-permute-start(f32[26,16,128]{2,1,0:T(8,128)} %shard_map.148.refs_0_), channel_id=1, source_target_pairs={{0,2},{2,0},{1,3},{3,1},{4,6},{6,4},{5,7},{7,5},{8,10},{10,8},{9,1... | collective-permute-start | bytes 638984 | tf_op jit(solution)/shard_map/ppermute | solution.py:60
  9.4 0.9 %slice_bitcast_fusion.7 = f32[1,10,16,128]{3,2,1,0:T(8,128)S(1)} fusion(f32[26,16,128]{2,1,0:T(8,128)} %shard_map.148.refs_0_), kind=kLoop, calls=%fused_computation.9 | loop fusion | bytes 163840 | tf_op jit(solution)/shard_map/stack | solution.py:299
  10.3 6.1 %collective-permute-done.2.refs_3_ = f32[26,16,128]{2,1,0:T(8,128)S(1)} collective-permute-done((f32[26,16,128]{2,1,0:T(8,128)}, f32[26,16,128]{2,1,0:T(8,128)S(1)}, u32[]{:S(2)}, u32[]{:S(2)}) %collective-permute-start.2) | collective-permute-done | bytes 213024 | tf_op jit(solution)/shard_map/ppermute | solution.py:60
  16.5 0.7 %collective-permute-start.3 = (f32[26,16,128]{2,1,0:T(8,128)S(1)}, f32[26,16,128]{2,1,0:T(8,128)S(1)}, u32[]{:S(2)}, u32[]{:S(2)}) collective-permute-start(f32[26,16,128]{2,1,0:T(8,128)S(1)} %collective-permute-done.2.refs_3_), channel_id=1, source_target_pairs={{0,4},{4,0},{8,12},{12,8},{1,5},{5,1},{9,13},{13,9},{2,6},{6,2},{1... | collective-permute-start | bytes 638984 | tf_op jit(solution)/shard_map/ppermute | solution.py:60
  17.3 0.1 collective-permute-start.7
  17.4 1.6 %collective-permute-start.5 = (f32[26,16,128]{2,1,0:T(8,128)S(1)}, f32[26,16,128]{2,1,0:T(8,128)S(1)}, u32[]{:S(2)}, u32[]{:S(2)}) collective-permute-start(f32[26,16,128]{2,1,0:T(8,128)S(1)} %collective-permute-done.2.refs_3_), channel_id=1, source_target_pairs={{0,2},{2,0},{1,3},{3,1},{4,6},{6,4},{5,7},{7,5},{8,10},{10,8},{9,1... | collective-permute-start | bytes 638984 | tf_op jit(solution)/shard_map/ppermute | solution.py:60
  18.9 1.4 %collective-permute-start.4 = (f32[26,16,128]{2,1,0:T(8,128)S(1)}, f32[26,16,128]{2,1,0:T(8,128)S(1)}, u32[]{:S(2)}, u32[]{:S(2)}) collective-permute-start(f32[26,16,128]{2,1,0:T(8,128)S(1)} %collective-permute-done.refs_1_), channel_id=1, source_target_pairs={{0,4},{4,0},{8,12},{12,8},{1,5},{5,1},{9,13},{13,9},{2,6},{6,2},{1... | collective-permute-start | bytes 638984 | tf_op jit(solution)/shard_map/ppermute | solution.py:60
  20.3 3.7 %collective-permute-done.3.refs_4_ = f32[26,16,128]{2,1,0:T(8,128)S(1)} collective-permute-done((f32[26,16,128]{2,1,0:T(8,128)S(1)}, f32[26,16,128]{2,1,0:T(8,128)S(1)}, u32[]{:S(2)}, u32[]{:S(2)}) %collective-permute-start.3) | collective-permute-done | bytes 213024 | tf_op jit(solution)/shard_map/ppermute | solution.py:60
  24.0 2.1 %collective-permute-start.6 = (f32[26,16,128]{2,1,0:T(8,128)S(1)}, f32[26,16,128]{2,1,0:T(8,128)S(1)}, u32[]{:S(2)}, u32[]{:S(2)}) collective-permute-start(f32[26,16,128]{2,1,0:T(8,128)S(1)} %collective-permute-done.3.refs_4_), channel_id=1, source_target_pairs={{0,2},{2,0},{1,3},{3,1},{4,6},{6,4},{5,7},{7,5},{8,10},{10,8},{9,1... | collective-permute-start | bytes 638984 | tf_op jit(solution)/shard_map/ppermute | solution.py:60
  26.1 1.3 %collective-permute-done.4.refs_5_ = f32[26,16,128]{2,1,0:T(8,128)S(1)} collective-permute-done((f32[26,16,128]{2,1,0:T(8,128)S(1)}, f32[26,16,128]{2,1,0:T(8,128)S(1)}, u32[]{:S(2)}, u32[]{:S(2)}) %collective-permute-start.4) | collective-permute-done | bytes 213024 | tf_op jit(solution)/shard_map/ppermute | solution.py:60
  27.4 2.5 %collective-permute-done.6.refs_7_ = f32[26,16,128]{2,1,0:T(8,128)S(1)} collective-permute-done((f32[26,16,128]{2,1,0:T(8,128)S(1)}, f32[26,16,128]{2,1,0:T(8,128)S(1)}, u32[]{:S(2)}, u32[]{:S(2)}) %collective-permute-start.6) | collective-permute-done | bytes 213024 | tf_op jit(solution)/shard_map/ppermute | solution.py:60
  29.9 0.0 copy-start.2
  29.9 0.0 copy-start.3
  29.9 0.0 copy-start.4
  30.0 0.1 collective-permute-start.8
  30.1 1.6 %collective-permute-done.8.refs_9_ = f32[4,10,16,128]{3,2,1,0:T(8,128)S(1)} collective-permute-done((f32[4,10,16,128]{3,2,1,0:T(8,128)S(1)}, f32[4,10,16,128]{3,2,1,0:T(8,128)S(1)}, u32[]{:S(2)}, u32[]{:S(2)}) %collective-permute-start.8) | collective-permute-done | bytes 327712 | tf_op jit(solution)/shard_map/ppermute | solution.py:60
  31.7 12.6 %shard_map.149 = (f32[1,4,16,128]{3,2,1,0:T(8,128)}, f32[1,4,16,128]{3,2,1,0:T(8,128)}, f32[4,12,16,128]{3,2,1,0:T(8,128)S(1)}) custom-call(s32[4]{0:T(128)S(1)} %copy-done.4, bf16[256,256]{1,0:T(8,128)(2,1)S(1)} %copy-done.3, bf16[256,256]{1,0:T(8,128)(2,1)S(1)} %copy-done.2, f32[26,16,128]{2,1,0:T(8,128)S(1)} %copy-done, ...), custom_call_target="tpu_custom_call" | custom-call | tf_op jit(solution)/shard_map/pallas_call | solution.py:306
  44.3 0.1 collective-permute-start.9
  44.4 1.6 %collective-permute-done.9.other_ref = f32[4,12,16,128]{3,2,1,0:T(8,128)S(1)} collective-permute-done((f32[4,12,16,128]{3,2,1,0:T(8,128)S(1)}, f32[4,12,16,128]{3,2,1,0:T(8,128)S(1)}, u32[]{:S(2)}, u32[]{:S(2)}) %collective-permute-start.9) | collective-permute-done | bytes 393248 | tf_op jit(solution)/shard_map/ppermute | solution.py:60
  46.0 0.8 %copy-done.5 = f32[4,12,16,128]{3,2,1,0:T(8,128)} copy-done((f32[4,12,16,128]{3,2,1,0:T(8,128)}, f32[4,12,16,128]{3,2,1,0:T(8,128)S(1)}, u32[]{:S(2)}) %copy-start.5) | copy-done | bytes 393240
  46.8 1.9 %shard_map.150 = f32[5,4,16,64]{3,2,1,0:T(8,128)} custom-call(s32[5]{0:T(128)} %lags_ref.1, f32[4,12,16,128]{3,2,1,0:T(8,128)} %copy-done.1, f32[4,12,16,128]{3,2,1,0:T(8,128)} %copy-done.5), custom_call_target="tpu_custom_call" | custom-call | tf_op jit(solution)/shard_map/pallas_call | solution.py:325
  (21 shorter events, 0.1 us)
Async XLA Ops:
  2.2 14.2 %collective-permute-start.2 = (f32[26,16,128]{2,1,0:T(8,128)}, f32[26,16,128]{2,1,0:T(8,128)S(1)}, u32[]{:S(2)}, u32[]{:S(2)}) collective-permute-start(f32[26,16,128]{2,1,0:T(8,128)} %shard_map.148.refs_0_), channel_id=1, source_target_pairs={{0,8},{4,12},{8,0},{12,4},{1,9},{5,13},{9,1},{13,5},{2,10},{6,14},... | collective-permute-start | bytes 638984 | tf_op jit(solution)/shard_map/ppermute | solution.py:60
  6.3 10.9 %collective-permute-start.1 = (f32[26,16,128]{2,1,0:T(8,128)}, f32[26,16,128]{2,1,0:T(8,128)S(1)}, u32[]{:S(2)}, u32[]{:S(2)}) collective-permute-start(f32[26,16,128]{2,1,0:T(8,128)} %shard_map.148.refs_0_), channel_id=1, source_target_pairs={{0,4},{4,0},{8,12},{12,8},{1,5},{5,1},{9,13},{13,9},{2,6},{6,2},{1... | collective-permute-start | bytes 638984 | tf_op jit(solution)/shard_map/ppermute | solution.py:60
  7.9 9.3 %collective-permute-start = (f32[26,16,128]{2,1,0:T(8,128)}, f32[26,16,128]{2,1,0:T(8,128)S(1)}, u32[]{:S(2)}, u32[]{:S(2)}) collective-permute-start(f32[26,16,128]{2,1,0:T(8,128)} %shard_map.148.refs_0_), channel_id=1, source_target_pairs={{0,2},{2,0},{1,3},{3,1},{4,6},{6,4},{5,7},{7,5},{8,10},{10,8},{9,1... | collective-permute-start | bytes 638984 | tf_op jit(solution)/shard_map/ppermute | solution.py:60
  16.5 7.5 %collective-permute-start.3 = (f32[26,16,128]{2,1,0:T(8,128)S(1)}, f32[26,16,128]{2,1,0:T(8,128)S(1)}, u32[]{:S(2)}, u32[]{:S(2)}) collective-permute-start(f32[26,16,128]{2,1,0:T(8,128)S(1)} %collective-permute-done.2.refs_3_), channel_id=1, source_target_pairs={{0,4},{4,0},{8,12},{12,8},{1,5},{5,1},{9,13},{13,9},{2,6},{6,2},{1... | collective-permute-start | bytes 638984 | tf_op jit(solution)/shard_map/ppermute | solution.py:60
  17.3 12.8 %collective-permute-start.7 = (f32[4,10,16,128]{3,2,1,0:T(8,128)S(1)}, f32[4,10,16,128]{3,2,1,0:T(8,128)S(1)}, u32[]{:S(2)}, u32[]{:S(2)}) collective-permute-start(f32[4,10,16,128]{3,2,1,0:T(8,128)S(1)} %pad_maximum_fusion), channel_id=1, source_target_pairs={{0,1},{1,0},{2,3},{3,2},{4,5},{5,4},{6,7},{7,6},{8,9},{9,8},{10,11... | collective-permute-start | bytes 983048 | tf_op jit(solution)/shard_map/ppermute | solution.py:60
  17.4 8.7 %collective-permute-start.5 = (f32[26,16,128]{2,1,0:T(8,128)S(1)}, f32[26,16,128]{2,1,0:T(8,128)S(1)}, u32[]{:S(2)}, u32[]{:S(2)}) collective-permute-start(f32[26,16,128]{2,1,0:T(8,128)S(1)} %collective-permute-done.2.refs_3_), channel_id=1, source_target_pairs={{0,2},{2,0},{1,3},{3,1},{4,6},{6,4},{5,7},{7,5},{8,10},{10,8},{9,1... | collective-permute-start | bytes 638984 | tf_op jit(solution)/shard_map/ppermute | solution.py:60
  18.9 8.5 %collective-permute-start.4 = (f32[26,16,128]{2,1,0:T(8,128)S(1)}, f32[26,16,128]{2,1,0:T(8,128)S(1)}, u32[]{:S(2)}, u32[]{:S(2)}) collective-permute-start(f32[26,16,128]{2,1,0:T(8,128)S(1)} %collective-permute-done.refs_1_), channel_id=1, source_target_pairs={{0,4},{4,0},{8,12},{12,8},{1,5},{5,1},{9,13},{13,9},{2,6},{6,2},{1... | collective-permute-start | bytes 638984 | tf_op jit(solution)/shard_map/ppermute | solution.py:60
  24.0 5.9 %collective-permute-start.6 = (f32[26,16,128]{2,1,0:T(8,128)S(1)}, f32[26,16,128]{2,1,0:T(8,128)S(1)}, u32[]{:S(2)}, u32[]{:S(2)}) collective-permute-start(f32[26,16,128]{2,1,0:T(8,128)S(1)} %collective-permute-done.3.refs_4_), channel_id=1, source_target_pairs={{0,2},{2,0},{1,3},{3,1},{4,6},{6,4},{5,7},{7,5},{8,10},{10,8},{9,1... | collective-permute-start | bytes 638984 | tf_op jit(solution)/shard_map/ppermute | solution.py:60
  29.9 1.8 %copy-start = (f32[26,16,128]{2,1,0:T(8,128)S(1)}, f32[26,16,128]{2,1,0:T(8,128)}, u32[]{:S(2)}) copy-start(f32[26,16,128]{2,1,0:T(8,128)} %shard_map.148.refs_0_) | copy-start | bytes 638980
  29.9 1.8 %copy-start.2 = (bf16[256,256]{1,0:T(8,128)(2,1)S(1)}, bf16[256,256]{1,0:T(8,128)(2,1)}, u32[]{:S(2)}) copy-start(bf16[256,256]{1,0:T(8,128)(2,1)} %constant.5.clone.lateral_ref) | copy-start | bytes 393220
  29.9 1.8 %copy-start.3 = (bf16[256,256]{1,0:T(8,128)(2,1)S(1)}, bf16[256,256]{1,0:T(8,128)(2,1)}, u32[]{:S(2)}) copy-start(bf16[256,256]{1,0:T(8,128)(2,1)} %constant.4.clone.depth_ref) | copy-start | bytes 393220
  29.9 1.8 %copy-start.4 = (s32[4]{0:T(128)S(1)}, s32[4]{0:T(128)}, u32[]{:S(2)}) copy-start(s32[4]{0:T(128)} %plan_ref.1) | copy-start | bytes 52
  30.0 1.7 %collective-permute-start.8 = (f32[4,10,16,128]{3,2,1,0:T(8,128)S(1)}, f32[4,10,16,128]{3,2,1,0:T(8,128)S(1)}, u32[]{:S(2)}, u32[]{:S(2)}) collective-permute-start(f32[4,10,16,128]{3,2,1,0:T(8,128)S(1)} %pad_maximum_fusion.1), channel_id=1, source_target_pairs={{0,1},{1,0},{2,3},{3,2},{4,5},{5,4},{6,7},{7,6},{8,9},{9,8},{10,11... | collective-permute-start | bytes 983048 | tf_op jit(solution)/shard_map/ppermute | solution.py:60
  44.3 1.7 %copy-start.1 = (f32[4,12,16,128]{3,2,1,0:T(8,128)}, f32[4,12,16,128]{3,2,1,0:T(8,128)S(1)}, u32[]{:S(2)}) copy-start(f32[4,12,16,128]{3,2,1,0:T(8,128)S(1)} %get-tuple-element.8.own_ref) | copy-start | bytes 1179652
  44.3 1.7 %collective-permute-start.9 = (f32[4,12,16,128]{3,2,1,0:T(8,128)S(1)}, f32[4,12,16,128]{3,2,1,0:T(8,128)S(1)}, u32[]{:S(2)}, u32[]{:S(2)}) collective-permute-start(f32[4,12,16,128]{3,2,1,0:T(8,128)S(1)} %get-tuple-element.8.own_ref), channel_id=1, source_target_pairs={{0,1},{1,0},{2,3},{3,2},{4,5},{5,4},{6,7},{7,6},{8,9},{9,8},{10,11... | collective-permute-start | bytes 1179656 | tf_op jit(solution)/shard_map/ppermute | solution.py:60
  46.0 0.8 %copy-start.5 = (f32[4,12,16,128]{3,2,1,0:T(8,128)}, f32[4,12,16,128]{3,2,1,0:T(8,128)S(1)}, u32[]{:S(2)}) copy-start(f32[4,12,16,128]{3,2,1,0:T(8,128)S(1)} %collective-permute-done.9.other_ref) | copy-start | bytes 1179652

commit v3 on v2

--- a/solution.py
+++ b/solution.py
@@ -242,19 +242,26 @@
     q_out[0] = now[0][1][pl.ds(gx * tile_x + REACH, tile_x), mine]
 
 
-def image_kernel(lags_ref, own_ref, other_ref, image_ref):
+def image_kernel(numbers_ref, own_ref, other_ref, p_ref, q_ref, p_out, q_out, image_ref, sems):
+    copies = [
+        pltpu.make_async_copy(a, b, sems.at[i]) for i, (a, b) in enumerate(((p_ref, p_out), (q_ref, q_out)))
+    ]
+    for copy in copies:
+        copy.start()
     sec = lax.axis_index("sec")
     sign = 1 - 2 * sec
     nlag, tile_x, tile_y, half = image_ref.shape
     nsnap = own_ref.shape[0]
     for k in range(nlag):
-        shift = sign * lags_ref[k]
+        shift = sign * numbers_ref[nsnap + k]
         total = own_ref[0, pl.ds(REACH - shift, tile_x)] * other_ref[0, pl.ds(REACH + shift, tile_x)]
         for j in range(1, nsnap):
             total = total + own_ref[j, pl.ds(REACH - shift, tile_x)] * other_ref[j, pl.ds(REACH + shift, tile_x)]
         flat = total.reshape(tile_x * tile_y, 2 * half)
         chosen = jnp.where(sec == 0, flat, pltpu.roll(flat, half, 1))
         image_ref[k] = chosen[:, :half].reshape(tile_x, tile_y, half)
+    for copy in copies:
+        copy.wait()
 
 
 def gathered_solution(pressure, pressure_before, quasi, quasi_before, courant, epsilon, delta, tilt, azimuth, plan, lags):
@@ -298,12 +305,13 @@
     tiles = [held[s] for s in slots]
     others = [swapped(jnp.stack([held[s][4 * tile_x :] for s in part]), "sec", 1) for part in (direct, relayed)]
 
+    numbers = jnp.concatenate([plan, lags])
     nsnap = plan.shape[0]
     sizes = (tile_x, tile_y, total_x, total_y, depth, slots, nsnap)
     field = pltpu.VMEM((total_x + 2 * REACH, total_y, depth), jnp.float32)
     slope = pltpu.VMEM((2, 2, total_x + 2 * REACH, total_y, depth), jnp.float32)
     rest = pltpu.VMEM((3, 2, total_x, total_y, depth), jnp.float32)
-    p_final, q_final, snaps = pl.pallas_call(
+    p_last, q_last, snaps = pl.pallas_call(
         functools.partial(steps_kernel, sizes),
         out_shape=(
             jax.ShapeDtypeStruct(pressure.shape, jnp.float32),
@@ -319,15 +327,21 @@
             pltpu.VMEM((nsnap + 1, tile_x + 2 * REACH, tile_y, depth), jnp.float32),
         ],
         compiler_params=pltpu.CompilerParams(vmem_limit_bytes=24 * 1024 * 1024),
-    )(plan, depth_matrix(depth), lateral_matrix(total_y), *tiles, *others)
+    )(numbers, depth_matrix(depth), lateral_matrix(total_y), *tiles, *others)
 
     other_snaps = swapped(snaps, "sec", 1)
-    image = pl.pallas_call(
+    p_final, q_final, image = pl.pallas_call(
         image_kernel,
-        out_shape=jax.ShapeDtypeStruct((lags.shape[0], tile_x, tile_y, depth // 2), jnp.float32),
-        in_specs=[smem, vmem, vmem],
-        out_specs=vmem,
-    )(lags, snaps, other_snaps)
+        out_shape=(
+            jax.ShapeDtypeStruct(pressure.shape, jnp.float32),
+            jax.ShapeDtypeStruct(quasi.shape, jnp.float32),
+            jax.ShapeDtypeStruct((lags.shape[0], tile_x, tile_y, depth // 2), jnp.float32),
+        ),
+        in_specs=[smem] + [vmem] * 4,
+        out_specs=(apart, apart, vmem),
+        scratch_shapes=[pltpu.SemaphoreType.DMA((2,))],
+        compiler_params=pltpu.CompilerParams(vmem_limit_bytes=8 * 1024 * 1024),
+    )(numbers, snaps, other_snaps, p_last, q_last)
     return (p_final, q_final, image)
 
 

time: 48.9 us -> 47.2 us (0.965)
  Pallas kernels: 16.1 us -> 15.1 us
  waiting for transfers between devices: 16.8 us -> 16.3 us
    pallas_call x1, Pallas kernels: 12.6 us -> 11.6 us  [gathered_solution(): pl.pallas_call(functools.partial(steps_kernel, sizes), out_shape=(jax.Sha...]
    ppermute x10, waiting for transfers between devices: 16.8 us -> 16.3 us  [swapped(): return lax.ppermute(block, axis, [(i, i ^ bit) for i in range(count)])]
where the time goes in v3:
time: 47.2 us; the launch traced here: 47 us
  waiting for transfers between devices  16.3 us (35%)
  Pallas kernels  15.1 us (32%)
  starting transfers between devices  13.2 us (28%)
  local copies, waits for them, and re-layouts  1.5 us (3%)
  between operations  0.77 us (2%)
    ppermute x10, waiting for transfers between devices, swapped(): return lax.ppermute(block, axis, [(i, i ^ bit) for i in range(count)])  16.3 us
    ppermute x10, starting transfers between devices, swapped(): return lax.ppermute(block, axis, [(i, i ^ bit) for i in range(count)])  13.2 us
    pallas_call x1, Pallas kernels, gathered_solution(): pl.pallas_call(functools.partial(steps_kernel, sizes), out_shape=(jax.Sha...  11.6 us
    pallas_call x1, Pallas kernels, gathered_solution(): pl.pallas_call(image_kernel, out_shape=(jax.ShapeDtypeStruct(pressure.sha...  1.87 us
    pallas_call x1, Pallas kernels, gathered_solution(): pl.pallas_call(pack_kernel, out_shape=jax.ShapeDtypeStruct((4 * tile_x +...  1.61 us
    another operation x8, local copies, waits for them, and re-layouts, gathered_solution(): jnp.stack([held[s][4 * tile_x:] for s in part])  0.97 us
  transfers between devices with their start and end apart: 10, of which 6 were waited for; matrix products, arithmetic and copies ran while one was open for 2% of the time, Pallas kernels for 0%

profile of v3, /device:TPU:0, one launch (start us, length us, event | category | flops | bytes accessed | tf_op | source)
XLA Modules:
  0.0 47.0 jit_solution(15476846720922800144)
XLA Ops:
  0.6 1.6 %shard_map.148.refs_0_ = f32[26,16,128]{2,1,0:T(8,128)} custom-call(f32[1,4,16,128]{3,2,1,0:T(8,128)} %refs_0_.1, f32[1,4,16,128]{3,2,1,0:T(8,128)} %refs_1_.1, f32[1,4,16,128]{3,2,1,0:T(8,128)} %refs_2_.1, f32[1,4,16,128]{3,2,1,0:T(8,128)} %refs_3_.1, f32[4,16,128]{2,1,0:T(8,128)} %refs_4_.1, f32[4,16,128]{2,1,0:T(8,128)} %refs_5_.1, ...), custom_call_target="tpu_custom_call" | custom-call | tf_op jit(solution)/shard_map/pallas_call | solution.py:277
  2.3 4.1 %collective-permute-start.2 = (f32[26,16,128]{2,1,0:T(8,128)}, f32[26,16,128]{2,1,0:T(8,128)S(1)}, u32[]{:S(2)}, u32[]{:S(2)}) collective-permute-start(f32[26,16,128]{2,1,0:T(8,128)} %shard_map.148.refs_0_), channel_id=1, source_target_pairs={{0,8},{4,12},{8,0},{12,4},{1,9},{5,13},{9,1},{13,5},{2,10},{6,14},... | collective-permute-start | bytes 638984 | tf_op jit(solution)/shard_map/ppermute | solution.py:60
  6.4 1.6 %collective-permute-start.1 = (f32[26,16,128]{2,1,0:T(8,128)}, f32[26,16,128]{2,1,0:T(8,128)S(1)}, u32[]{:S(2)}, u32[]{:S(2)}) collective-permute-start(f32[26,16,128]{2,1,0:T(8,128)} %shard_map.148.refs_0_), channel_id=1, source_target_pairs={{0,4},{4,0},{8,12},{12,8},{1,5},{5,1},{9,13},{13,9},{2,6},{6,2},{1... | collective-permute-start | bytes 638984 | tf_op jit(solution)/shard_map/ppermute | solution.py:60
  7.9 1.5 %collective-permute-start = (f32[26,16,128]{2,1,0:T(8,128)}, f32[26,16,128]{2,1,0:T(8,128)S(1)}, u32[]{:S(2)}, u32[]{:S(2)}) collective-permute-start(f32[26,16,128]{2,1,0:T(8,128)} %shard_map.148.refs_0_), channel_id=1, source_target_pairs={{0,2},{2,0},{1,3},{3,1},{4,6},{6,4},{5,7},{7,5},{8,10},{10,8},{9,1... | collective-permute-start | bytes 638984 | tf_op jit(solution)/shard_map/ppermute | solution.py:60
  9.4 0.9 %slice_bitcast_fusion.7 = f32[1,10,16,128]{3,2,1,0:T(8,128)S(1)} fusion(f32[26,16,128]{2,1,0:T(8,128)} %shard_map.148.refs_0_), kind=kLoop, calls=%fused_computation.9 | loop fusion | bytes 163840 | tf_op jit(solution)/shard_map/stack | solution.py:306
  10.3 6.1 %collective-permute-done.2.refs_3_ = f32[26,16,128]{2,1,0:T(8,128)S(1)} collective-permute-done((f32[26,16,128]{2,1,0:T(8,128)}, f32[26,16,128]{2,1,0:T(8,128)S(1)}, u32[]{:S(2)}, u32[]{:S(2)}) %collective-permute-start.2) | collective-permute-done | bytes 213024 | tf_op jit(solution)/shard_map/ppermute | solution.py:60
  16.5 0.7 %collective-permute-start.3 = (f32[26,16,128]{2,1,0:T(8,128)S(1)}, f32[26,16,128]{2,1,0:T(8,128)S(1)}, u32[]{:S(2)}, u32[]{:S(2)}) collective-permute-start(f32[26,16,128]{2,1,0:T(8,128)S(1)} %collective-permute-done.2.refs_3_), channel_id=1, source_target_pairs={{0,4},{4,0},{8,12},{12,8},{1,5},{5,1},{9,13},{13,9},{2,6},{6,2},{1... | collective-permute-start | bytes 638984 | tf_op jit(solution)/shard_map/ppermute | solution.py:60
  17.3 0.1 collective-permute-start.7
  17.4 1.6 %collective-permute-start.5 = (f32[26,16,128]{2,1,0:T(8,128)S(1)}, f32[26,16,128]{2,1,0:T(8,128)S(1)}, u32[]{:S(2)}, u32[]{:S(2)}) collective-permute-start(f32[26,16,128]{2,1,0:T(8,128)S(1)} %collective-permute-done.2.refs_3_), channel_id=1, source_target_pairs={{0,2},{2,0},{1,3},{3,1},{4,6},{6,4},{5,7},{7,5},{8,10},{10,8},{9,1... | collective-permute-start | bytes 638984 | tf_op jit(solution)/shard_map/ppermute | solution.py:60
  18.9 1.4 %collective-permute-start.4 = (f32[26,16,128]{2,1,0:T(8,128)S(1)}, f32[26,16,128]{2,1,0:T(8,128)S(1)}, u32[]{:S(2)}, u32[]{:S(2)}) collective-permute-start(f32[26,16,128]{2,1,0:T(8,128)S(1)} %collective-permute-done.refs_1_), channel_id=1, source_target_pairs={{0,4},{4,0},{8,12},{12,8},{1,5},{5,1},{9,13},{13,9},{2,6},{6,2},{1... | collective-permute-start | bytes 638984 | tf_op jit(solution)/shard_map/ppermute | solution.py:60
  20.3 3.7 %collective-permute-done.3.refs_4_ = f32[26,16,128]{2,1,0:T(8,128)S(1)} collective-permute-done((f32[26,16,128]{2,1,0:T(8,128)S(1)}, f32[26,16,128]{2,1,0:T(8,128)S(1)}, u32[]{:S(2)}, u32[]{:S(2)}) %collective-permute-start.3) | collective-permute-done | bytes 213024 | tf_op jit(solution)/shard_map/ppermute | solution.py:60
  24.0 2.1 %collective-permute-start.6 = (f32[26,16,128]{2,1,0:T(8,128)S(1)}, f32[26,16,128]{2,1,0:T(8,128)S(1)}, u32[]{:S(2)}, u32[]{:S(2)}) collective-permute-start(f32[26,16,128]{2,1,0:T(8,128)S(1)} %collective-permute-done.3.refs_4_), channel_id=1, source_target_pairs={{0,2},{2,0},{1,3},{3,1},{4,6},{6,4},{5,7},{7,5},{8,10},{10,8},{9,1... | collective-permute-start | bytes 638984 | tf_op jit(solution)/shard_map/ppermute | solution.py:60
  26.1 1.3 %collective-permute-done.4.refs_5_ = f32[26,16,128]{2,1,0:T(8,128)S(1)} collective-permute-done((f32[26,16,128]{2,1,0:T(8,128)S(1)}, f32[26,16,128]{2,1,0:T(8,128)S(1)}, u32[]{:S(2)}, u32[]{:S(2)}) %collective-permute-start.4) | collective-permute-done | bytes 213024 | tf_op jit(solution)/shard_map/ppermute | solution.py:60
  27.4 2.5 %collective-permute-done.6.refs_7_ = f32[26,16,128]{2,1,0:T(8,128)S(1)} collective-permute-done((f32[26,16,128]{2,1,0:T(8,128)S(1)}, f32[26,16,128]{2,1,0:T(8,128)S(1)}, u32[]{:S(2)}, u32[]{:S(2)}) %collective-permute-start.6) | collective-permute-done | bytes 213024 | tf_op jit(solution)/shard_map/ppermute | solution.py:60
  29.9 0.0 copy-start.1
  30.0 0.1 collective-permute-start.8
  30.1 0.5 %copy-done.3 = s32[5]{0:T(128)S(1)} copy-done((s32[5]{0:T(128)S(1)}, s32[5]{0:T(128)}, u32[]{:S(2)}) %copy-start.3) | copy-done | bytes 44
  30.6 0.0 copy-done.4
  30.6 0.1 pad_add_fusion.plan_ref.numbers_ref
  30.7 1.0 %collective-permute-done.8.refs_9_ = f32[4,10,16,128]{3,2,1,0:T(8,128)S(1)} collective-permute-done((f32[4,10,16,128]{3,2,1,0:T(8,128)S(1)}, f32[4,10,16,128]{3,2,1,0:T(8,128)S(1)}, u32[]{:S(2)}, u32[]{:S(2)}) %collective-permute-start.8) | collective-permute-done | bytes 327712 | tf_op jit(solution)/shard_map/ppermute | solution.py:60
  31.7 11.6 %shard_map.149 = (f32[1,4,16,128]{3,2,1,0:T(8,128)S(1)}, f32[1,4,16,128]{3,2,1,0:T(8,128)S(1)}, f32[4,12,16,128]{3,2,1,0:T(8,128)S(1)}) custom-call(s32[9]{0:T(128)S(1)} %pad_add_fusion.plan_ref.numbers_ref, bf16[256,256]{1,0:T(8,128)(2,1)S(1)} %copy-done.2, bf16[256,256]{1,0:T(8,128)(2,1)S(1)} %copy-done.1, f32[26,16,128]{2,1,0:T(8,128)S(1)} %copy-done, ...), custom_call_target="tpu_custom_call" | custom-call | tf_op jit(solution)/shard_map/pallas_call | solution.py:314
  43.3 0.2 collective-permute-start.9
  43.5 1.6 %collective-permute-done.9.other_ref = f32[4,12,16,128]{3,2,1,0:T(8,128)S(1)} collective-permute-done((f32[4,12,16,128]{3,2,1,0:T(8,128)S(1)}, f32[4,12,16,128]{3,2,1,0:T(8,128)S(1)}, u32[]{:S(2)}, u32[]{:S(2)}) %collective-permute-start.9) | collective-permute-done | bytes 393248 | tf_op jit(solution)/shard_map/ppermute | solution.py:60
  45.1 1.9 %shard_map.150 = (f32[1,4,16,128]{3,2,1,0:T(8,128)}, f32[1,4,16,128]{3,2,1,0:T(8,128)}, f32[5,4,16,64]{3,2,1,0:T(8,128)}) custom-call(s32[9]{0:T(128)S(1)} %pad_add_fusion.plan_ref.numbers_ref, f32[4,12,16,128]{3,2,1,0:T(8,128)S(1)} %get-tuple-element.6.own_ref, f32[4,12,16,128]{3,2,1,0:T(8,128)S(1)} %collective-permute-done.9.other_ref, ...), custom_call_target="tpu_custom_call" | custom-call | tf_op jit(solution)/shard_map/pallas_call | solution.py:333
  (20 shorter events, 0.1 us)
Async XLA Ops:
  2.3 14.2 %collective-permute-start.2 = (f32[26,16,128]{2,1,0:T(8,128)}, f32[26,16,128]{2,1,0:T(8,128)S(1)}, u32[]{:S(2)}, u32[]{:S(2)}) collective-permute-start(f32[26,16,128]{2,1,0:T(8,128)} %shard_map.148.refs_0_), channel_id=1, source_target_pairs={{0,8},{4,12},{8,0},{12,4},{1,9},{5,13},{9,1},{13,5},{2,10},{6,14},... | collective-permute-start | bytes 638984 | tf_op jit(solution)/shard_map/ppermute | solution.py:60
  6.4 10.9 %collective-permute-start.1 = (f32[26,16,128]{2,1,0:T(8,128)}, f32[26,16,128]{2,1,0:T(8,128)S(1)}, u32[]{:S(2)}, u32[]{:S(2)}) collective-permute-start(f32[26,16,128]{2,1,0:T(8,128)} %shard_map.148.refs_0_), channel_id=1, source_target_pairs={{0,4},{4,0},{8,12},{12,8},{1,5},{5,1},{9,13},{13,9},{2,6},{6,2},{1... | collective-permute-start | bytes 638984 | tf_op jit(solution)/shard_map/ppermute | solution.py:60
  7.9 9.3 %collective-permute-start = (f32[26,16,128]{2,1,0:T(8,128)}, f32[26,16,128]{2,1,0:T(8,128)S(1)}, u32[]{:S(2)}, u32[]{:S(2)}) collective-permute-start(f32[26,16,128]{2,1,0:T(8,128)} %shard_map.148.refs_0_), channel_id=1, source_target_pairs={{0,2},{2,0},{1,3},{3,1},{4,6},{6,4},{5,7},{7,5},{8,10},{10,8},{9,1... | collective-permute-start | bytes 638984 | tf_op jit(solution)/shard_map/ppermute | solution.py:60
  16.5 7.5 %collective-permute-start.3 = (f32[26,16,128]{2,1,0:T(8,128)S(1)}, f32[26,16,128]{2,1,0:T(8,128)S(1)}, u32[]{:S(2)}, u32[]{:S(2)}) collective-permute-start(f32[26,16,128]{2,1,0:T(8,128)S(1)} %collective-permute-done.2.refs_3_), channel_id=1, source_target_pairs={{0,4},{4,0},{8,12},{12,8},{1,5},{5,1},{9,13},{13,9},{2,6},{6,2},{1... | collective-permute-start | bytes 638984 | tf_op jit(solution)/shard_map/ppermute | solution.py:60
  17.3 13.4 %collective-permute-start.7 = (f32[4,10,16,128]{3,2,1,0:T(8,128)S(1)}, f32[4,10,16,128]{3,2,1,0:T(8,128)S(1)}, u32[]{:S(2)}, u32[]{:S(2)}) collective-permute-start(f32[4,10,16,128]{3,2,1,0:T(8,128)S(1)} %pad_maximum_fusion), channel_id=1, source_target_pairs={{0,1},{1,0},{2,3},{3,2},{4,5},{5,4},{6,7},{7,6},{8,9},{9,8},{10,11... | collective-permute-start | bytes 983048 | tf_op jit(solution)/shard_map/ppermute | solution.py:60
  17.4 8.7 %collective-permute-start.5 = (f32[26,16,128]{2,1,0:T(8,128)S(1)}, f32[26,16,128]{2,1,0:T(8,128)S(1)}, u32[]{:S(2)}, u32[]{:S(2)}) collective-permute-start(f32[26,16,128]{2,1,0:T(8,128)S(1)} %collective-permute-done.2.refs_3_), channel_id=1, source_target_pairs={{0,2},{2,0},{1,3},{3,1},{4,6},{6,4},{5,7},{7,5},{8,10},{10,8},{9,1... | collective-permute-start | bytes 638984 | tf_op jit(solution)/shard_map/ppermute | solution.py:60
  18.9 8.5 %collective-permute-start.4 = (f32[26,16,128]{2,1,0:T(8,128)S(1)}, f32[26,16,128]{2,1,0:T(8,128)S(1)}, u32[]{:S(2)}, u32[]{:S(2)}) collective-permute-start(f32[26,16,128]{2,1,0:T(8,128)S(1)} %collective-permute-done.refs_1_), channel_id=1, source_target_pairs={{0,4},{4,0},{8,12},{12,8},{1,5},{5,1},{9,13},{13,9},{2,6},{6,2},{1... | collective-permute-start | bytes 638984 | tf_op jit(solution)/shard_map/ppermute | solution.py:60
  24.0 5.9 %collective-permute-start.6 = (f32[26,16,128]{2,1,0:T(8,128)S(1)}, f32[26,16,128]{2,1,0:T(8,128)S(1)}, u32[]{:S(2)}, u32[]{:S(2)}) collective-permute-start(f32[26,16,128]{2,1,0:T(8,128)S(1)} %collective-permute-done.3.refs_4_), channel_id=1, source_target_pairs={{0,2},{2,0},{1,3},{3,1},{4,6},{6,4},{5,7},{7,5},{8,10},{10,8},{9,1... | collective-permute-start | bytes 638984 | tf_op jit(solution)/shard_map/ppermute | solution.py:60
  29.9 0.7 %copy-start.3 = (s32[5]{0:T(128)S(1)}, s32[5]{0:T(128)}, u32[]{:S(2)}) copy-start(s32[5]{0:T(128)} %param.23) | copy-start | bytes 64
  29.9 0.7 %copy-start.4 = (s32[4]{0:T(128)S(1)}, s32[4]{0:T(128)}, u32[]{:S(2)}) copy-start(s32[4]{0:T(128)} %param.22) | copy-start | bytes 52
  29.9 1.8 %copy-start = (f32[26,16,128]{2,1,0:T(8,128)S(1)}, f32[26,16,128]{2,1,0:T(8,128)}, u32[]{:S(2)}) copy-start(f32[26,16,128]{2,1,0:T(8,128)} %shard_map.148.refs_0_) | copy-start | bytes 638980
  29.9 1.8 %copy-start.1 = (bf16[256,256]{1,0:T(8,128)(2,1)S(1)}, bf16[256,256]{1,0:T(8,128)(2,1)}, u32[]{:S(2)}) copy-start(bf16[256,256]{1,0:T(8,128)(2,1)} %constant.5.clone.lateral_ref) | copy-start | bytes 393220
  30.0 1.7 %copy-start.2 = (bf16[256,256]{1,0:T(8,128)(2,1)S(1)}, bf16[256,256]{1,0:T(8,128)(2,1)}, u32[]{:S(2)}) copy-start(bf16[256,256]{1,0:T(8,128)(2,1)} %constant.4.clone.depth_ref) | copy-start | bytes 393220
  30.0 1.7 %collective-permute-start.8 = (f32[4,10,16,128]{3,2,1,0:T(8,128)S(1)}, f32[4,10,16,128]{3,2,1,0:T(8,128)S(1)}, u32[]{:S(2)}, u32[]{:S(2)}) collective-permute-start(f32[4,10,16,128]{3,2,1,0:T(8,128)S(1)} %pad_maximum_fusion.1), channel_id=1, source_target_pairs={{0,1},{1,0},{2,3},{3,2},{4,5},{5,4},{6,7},{7,6},{8,9},{9,8},{10,11... | collective-permute-start | bytes 983048 | tf_op jit(solution)/shard_map/ppermute | solution.py:60
  43.3 1.8 %collective-permute-start.9 = (f32[4,12,16,128]{3,2,1,0:T(8,128)S(1)}, f32[4,12,16,128]{3,2,1,0:T(8,128)S(1)}, u32[]{:S(2)}, u32[]{:S(2)}) collective-permute-start(f32[4,12,16,128]{3,2,1,0:T(8,128)S(1)} %get-tuple-element.6.own_ref), channel_id=1, source_target_pairs={{0,1},{1,0},{2,3},{3,2},{4,5},{5,4},{6,7},{7,6},{8,9},{9,8},{10,11... | collective-permute-start | bytes 1179656 | tf_op jit(solution)/shard_map/ppermute | solution.py:60
